TPU v7x, 768 devices: a whole 4x8x12 slice. The times are simulated.
768 devices in a mesh: gx: 96 (over x, z, core), gy: 8 (over y).
Axes of the slice: x: 4, y: 8, z: 12, core: 2. Of those that a mesh axis runs over, the one named last changes fastest.
Arguments:
- fields: bfloat16 [4, 6144, 1024], P(None, 'gx', 'gy'), may hold values from -6 to 6
- ocean_mask: int32 [6144, 1024], P('gx', 'gy'), may hold values from 0 to 1, as said below
- metric: float32 [2, 1024], P(None, 'gy'), may hold values from 1 to 4
- w_first: bfloat16 [5, 48, 4], replicated, may hold values from -1.5 to 1.5
- w_mid: bfloat16 [3, 5, 48, 48], replicated, may hold values from -0.4375 to 0.4375
- w_last: bfloat16 [5, 3, 48], replicated, may hold values from -0.4375 to 0.4375
- biases: float32 [4, 48], replicated, may hold values from -1.5 to 1.5
Outputs:
- forcing: float32 [2, 6144, 1024], P(None, 'gx', 'gy')
Inputs may be any that keep to these rules, and one draw needn't show every extreme that they name: ocean_mask is constant on aligned blocks of 4 x 4 cells.
All inputs are finite; a program needn't handle non-finite values.
Results may differ from a plain program's by a relative error of at most 0.006.
The roundings to bfloat16 on the way count: a program that leaves them out, or rounds other values in their place, can miss the bound.
Values may be sent and summed in bfloat16 or wider, within the bound.
No kernel may reach another device: no remote copies, remote signals or barrier semaphores. Data moves between devices by JAX's collectives and lax.ppermute only.
A program may use at most 32 MiB of HBM per device.

v0:
```python
import jax
import jax.numpy as jnp
from jax import lax
from jax.experimental import pallas as pl
from jax.experimental.pallas import tpu as pltpu
from jax.sharding import PartitionSpec as P

HALO = 8
BASE = 2 * HALO
ONES = 16
STRIP = 32
F32 = jnp.float32
BF16 = jnp.bfloat16
ALONG_X = (0, 1, 2, 3, 4)
ALONG_Y = (0, 3, 2, 1, 4)
VMEM = pl.BlockSpec(memory_space=pltpu.VMEM)


def iota(shape, dim):
    return lax.broadcasted_iota(jnp.int32, shape, dim)


def sides(fields, mask, got_in, got_out):
    chans = fields.shape[0] + 1
    odd = lax.rem(lax.axis_index("gx"), 2)
    west, own, east = [], [], []
    for c in range(chans):
        near = got_in[1 - odd, c]
        far = got_out[odd, c]
        near_low, near_high = near[:HALO].astype(F32), near[HALO:].astype(F32)
        far_low, far_high = far[:HALO].astype(F32), far[HALO:].astype(F32)
        west.append(jnp.where(odd == 1, near_high, far_high))
        east.append(jnp.where(odd == 1, far_low, near_low))
        own.append(fields[c].astype(F32) if c < chans - 1 else mask[...].astype(F32))
    return west, own, east


def pack_kernel(fields, mask, got_in, got_out, pay_in, pay_out, own_low, own_top):
    chans = fields.shape[0] + 1
    span_x, span_y = mask.shape
    wide = span_x + 2 * HALO
    lat, last = lax.axis_index("gy"), lax.axis_size("gy") - 1
    odd = lax.rem(lat, 2) == 1
    west, own, east = sides(fields, mask, got_in, got_out)
    pad = jnp.zeros((span_y - wide, span_y), F32)
    slot = 4 * HALO
    lane = iota((wide, span_y), 1)
    low, top = [], []
    for first in range(0, chans, span_y // slot):
        group = range(first, min(first + span_y // slot, chans))
        gathered = jnp.zeros((wide, span_y), F32)
        for i, c in enumerate(group):
            col = jnp.concatenate([west[c], own[c], east[c]], axis=0)
            here = (lane >= i * slot) & (lane < (i + 1) * slot)
            gathered = jnp.where(here, turn(col, i * slot + 2 * HALO), gathered)
        turned = jnp.concatenate([gathered, pad], axis=0).T
        for i, c in enumerate(group):
            own_top[c] = turned[i * slot : i * slot + 2 * HALO]
            own_low[c] = turned[i * slot + 2 * HALO : (i + 1) * slot]
            top.append(turned[i * slot + HALO : i * slot + 2 * HALO])
            low.append(turned[i * slot + 2 * HALO : i * slot + 3 * HALO])
    low = jnp.concatenate(low, axis=0)
    top = jnp.concatenate(top, axis=0)
    a, b = iota((span_y, span_y), 0), iota((span_y, span_y), 1)
    flip_x = (a + b == wide - 1).astype(BF16)
    a, b = iota((chans * HALO, chans * HALO), 0), iota((chans * HALO, chans * HALO), 1)
    flip_y = ((a // HALO == b // HALO) & (a % HALO + b % HALO == HALO - 1)).astype(BF16)
    mirrored = jnp.dot(top.astype(BF16), flip_x, preferred_element_type=F32).astype(BF16)
    mirrored = jnp.dot(flip_y, mirrored, preferred_element_type=F32)
    out_top = jnp.where(lat == last, mirrored, top)
    for c in range(chans):
        part = slice(c * HALO, (c + 1) * HALO)
        pay_in[c] = jnp.where(odd, low[part], top[part]).astype(BF16)
        pay_out[c] = jnp.where(odd, out_top[part], low[part]).astype(BF16)


def ones_rows(lanes):
    return (iota((ONES, lanes), 0) < 3).astype(BF16)


def turn(v, by):
    return pltpu.roll(v, by % v.shape[-1], v.ndim - 1)


def first_taps(window, order):
    pieces = [[] for _ in range(5)]
    for w in window:
        west, here, east = w[7:15], w[8:16], w[9:17]
        pieces[0].append(turn(west, 1) + turn(east, -1))
        pieces[1].append(west + east)
        pieces[2].append(turn(west, -1) + turn(east, 1))
        pieces[3].append(turn(here, 1) + turn(here, -1))
        pieces[4].append(here)
    stacked = jnp.concatenate([p for t in order for p in pieces[t]], axis=0).astype(BF16)
    return jnp.concatenate([stacked, ones_rows(stacked.shape[1])], axis=0)


def hidden_taps(load, row, order):
    parts = [
        load(1, row - 1) + load(2, row + 1),
        load(0, row - 1) + load(0, row + 1),
        load(2, row - 1) + load(1, row + 1),
        load(1, row) + load(2, row),
        load(0, row),
    ]
    return jnp.concatenate([parts[t] for t in order] + [ones_rows(parts[0].shape[1])], axis=0)


def loader(src):
    seen = {}

    def load(version, row):
        if (version, row) not in seen:
            seen[version, row] = src[version, row]
        return seen[version, row]

    return load


def activate(summed, ocean_row):
    ocean = jnp.broadcast_to(ocean_row, (16, ocean_row.shape[1])).astype(BF16)
    ocean = jnp.concatenate([ocean] * (summed.shape[0] // 16), axis=0)
    return jnp.maximum(summed.astype(BF16), jnp.zeros((), BF16)) * ocean


def put(dst, row, v):
    dst[0, row] = v
    dst[1, row] = turn(v, 1)
    dst[2, row] = turn(v, -1)


def bias_columns(biases, k):
    hid = biases.shape[1]
    a, b = iota((hid, hid), 0), iota((hid, hid), 1)
    row = jnp.broadcast_to(biases[k : k + 1, :], (hid, hid))
    rest = jnp.sum(jnp.where(a == b, row, 0.0), axis=1, keepdims=True)
    spread = jnp.zeros((hid, ONES), F32)
    at = iota((hid, ONES), 1)
    for i in range(3):
        piece = rest.astype(BF16).astype(F32)
        spread = jnp.where(at == i, jnp.broadcast_to(piece, (hid, ONES)), spread)
        rest = rest - piece
    return spread


def arrange_weights(w_first, w_mid, w_last, biases, big, hidden, final):
    taps, hid, feeds = w_first.shape
    n_mid = w_mid.shape[0]
    depth = taps * feeds * 8
    final[...] = jnp.zeros_like(final)
    spread = jnp.zeros((hid, depth), F32)
    for t in range(taps):
        a, b = iota((feeds, depth), 0), iota((feeds, depth), 1)
        place = (b // 8 == t * feeds + a).astype(BF16)
        spread = spread + jnp.dot(w_first[t], place, preferred_element_type=F32)
        final[: w_last.shape[1], t * hid : (t + 1) * hid] = w_last[t]
        for k in range(n_mid):
            hidden[k, :, t * hid : (t + 1) * hid] = w_mid[k, t]
    sub = iota((hid, depth), 1) % 8
    first_bias = bias_columns(biases, 0).astype(BF16)
    for r in range(8):
        big[r * hid : (r + 1) * hid, :depth] = jnp.where(sub == r, spread, 0.0).astype(BF16)
        big[r * hid : (r + 1) * hid, depth:] = first_bias
    for k in range(n_mid):
        hidden[k, :, taps * hid :] = bias_columns(biases, k + 1).astype(BF16)


def main_kernel(
    fields, mask, got_in, got_out, w_first, w_mid, w_last, biases, stress, big, hidden, final, ext, h_a, h_b
):
    chans = fields.shape[0] + 1
    feeds = chans - 1
    span_x, span_y = mask.shape
    n_mid, hid, _ = hidden.shape
    arrange_weights(w_first, w_mid, w_last, biases, big, hidden, final)
    west, own, east = sides(fields, mask, got_in, got_out)
    nothing = jnp.zeros((HALO, span_y), F32)
    for c in range(chans):
        ext[c, :HALO] = nothing
        ext[c, HALO:BASE] = west[c]
        ext[c, BASE : BASE + span_x] = own[c]
        ext[c, BASE + span_x : BASE + span_x + HALO] = east[c]
        ext[c, BASE + span_x + HALO :] = nothing

    def ocean_row(row):
        return ext[chans - 1, row : row + 1, :]

    def halves(v):
        return v[:, :span_y], v[:, span_y:]

    for start in range(HALO, BASE + span_x + HALO, 16):
        taps = [
            first_taps([ext[c, row - 8 : row + 16, :] for c in range(feeds)], ALONG_X)
            for row in (start, start + 8)
        ]
        summed = jnp.dot(big[...], jnp.concatenate(taps, axis=1), preferred_element_type=F32)
        for part, row in zip(halves(summed), (start, start + 8)):
            for r in range(8):
                put(h_a, row + r, activate(part[r * hid : (r + 1) * hid], ocean_row(row + r)))

    def layer(weights, src, reach, finish):
        cached = loader(src)
        for start in range(BASE - reach, BASE + span_x + reach, 2):
            taps = [hidden_taps(cached, row, ALONG_X) for row in (start, start + 1)]
            summed = jnp.dot(weights, jnp.concatenate(taps, axis=1), preferred_element_type=F32)
            for part, row in zip(halves(summed), (start, start + 1)):
                finish(part, row)

    src, dst = h_a, h_b
    for k in range(n_mid):
        layer(hidden[k], src, n_mid + 1 - k, lambda v, row: put(dst, row, activate(v, ocean_row(row))))
        src, dst = dst, src

    def finish(summed, row):
        v = (summed[:8] * ocean_row(row)).astype(BF16).astype(F32)
        for c in range(3):
            stress[c, row : row + 1, :] = v[c : c + 1]

    layer(final[...], src, 1, finish)


def strip_kernel(
    own_low, own_top, got_in, got_out, stress, big, hidden, final, mask, metric, out, ext, h_a, h_b, edge
):
    chans = own_low.shape[0]
    feeds = chans - 1
    span_x, span_y = mask.shape
    n_mid, hid, _ = hidden.shape
    odd = lax.rem(lax.axis_index("gy"), 2) == 1
    ext[...] = jnp.zeros_like(ext)
    for c in range(chans):
        inner, outer = got_in[c].astype(F32), got_out[c].astype(F32)
        below = jnp.where(odd, inner, outer)
        above = jnp.where(odd, outer, inner)
        ext[c, 6:14, :span_y] = below
        ext[c, 14:30, :span_y] = own_low[c]
        ext[c, 2:18, span_y:] = own_top[c]
        ext[c, 18:26, span_y:] = above

    def ocean_row(row):
        return ext[chans - 1, row : row + 1, :]

    def put_both(dst, row, v):
        for half in range(2):
            lanes = slice(half * span_y, (half + 1) * span_y)
            part = v[:, lanes]
            dst[0, row, :, lanes] = part
            dst[1, row, :, lanes] = turn(part, 1)
            dst[2, row, :, lanes] = turn(part, -1)

    for row in (8, 16):
        taps = [
            first_taps([ext[c, row - 8 : row + 16, half * span_y : (half + 1) * span_y] for c in range(feeds)], ALONG_Y)
            for half in range(2)
        ]
        summed = jnp.dot(big[...], jnp.concatenate(taps, axis=1), preferred_element_type=F32)
        for r in range(8):
            put_both(h_a, row + r, activate(summed[r * hid : (r + 1) * hid], ocean_row(row + r)))

    src, dst = h_a, h_b
    for k in range(n_mid):
        cached = loader(src)
        for row in range(10 + k, 22 - k):
            taps = hidden_taps(cached, row, ALONG_Y)
            summed = jnp.dot(hidden[k], taps, preferred_element_type=F32)
            put_both(dst, row, activate(summed, ocean_row(row)))
        src, dst = dst, src
    edge[...] = jnp.zeros_like(edge)
    cached = loader(src)
    for row in range(13, 19):
        summed = jnp.dot(final[...], hidden_taps(cached, row, ALONG_Y), preferred_element_type=F32)
        v = (summed[:8] * ocean_row(row)).astype(BF16).astype(F32)
        low, high = row - 14, span_y - 18 + row
        for c in range(3):
            for lat, part in ((low, v[c : c + 1, :span_y]), (high, v[c : c + 1, span_y:])):
                tile, slot = (0, lat) if 0 <= lat < span_y else (1, lat % span_y)
                edge[c, tile, slot : slot + 1, :] = part

    half_x = metric[0:1, :] * 0.5
    half_y = metric[1:2, :] * 0.5
    ocean = mask[...].astype(F32)
    lane = iota((span_x + 2, span_y), 1)
    planes, north, south = [], [], []
    for c in range(3):
        inside = edge[c, 0].T[HALO - 1 : HALO + span_x + 1]
        beyond = edge[c, 1].T[HALO : HALO + span_x]
        near = (lane < 5) | (lane >= span_y - 5)
        plane = jnp.where(near, inside, stress[c, BASE - 1 : BASE + span_x + 1, :])
        here = plane[1 : 1 + span_x]
        inner = lane[:span_x]
        planes.append(plane)
        north.append(turn(jnp.where(inner == 0, beyond, here), -1))
        south.append(turn(jnp.where(inner == span_y - 1, beyond, here), 1))

    def diff_x(c):
        return (planes[c][2:] - planes[c][:span_x]) * half_x

    def diff_y(c):
        return (north[c] - south[c]) * half_y

    out[0] = (diff_x(0) + diff_y(1)) * ocean
    out[1] = (diff_x(1) + diff_y(2)) * ocean


def pack(fields, mask, got_in, got_out):
    chans, span_y = fields.shape[0] + 1, mask.shape[1]
    return pl.pallas_call(
        pack_kernel,
        out_shape=[jax.ShapeDtypeStruct((chans, HALO, span_y), BF16)] * 2
        + [jax.ShapeDtypeStruct((chans, 2 * HALO, span_y), F32)] * 2,
        in_specs=[VMEM] * 4,
        out_specs=[VMEM] * 4,
        compiler_params=pltpu.CompilerParams(vmem_limit_bytes=4 * 1024 * 1024),
        name="pack_rows",
    )(fields, mask, got_in, got_out)


def main(fields, mask, got_in, got_out, w_first, w_mid, w_last, biases):
    span_x, span_y = mask.shape
    rows = span_x + 4 * HALO
    taps, hid, feeds = w_first.shape
    n_mid = w_mid.shape[0]
    return pl.pallas_call(
        main_kernel,
        out_shape=[
            jax.ShapeDtypeStruct((3, rows, span_y), F32),
            jax.ShapeDtypeStruct((8 * hid, taps * feeds * 8 + ONES), BF16),
            jax.ShapeDtypeStruct((n_mid, hid, taps * hid + ONES), BF16),
            jax.ShapeDtypeStruct((16, taps * hid + ONES), BF16),
        ],
        in_specs=[VMEM] * 8,
        out_specs=[VMEM] * 4,
        scratch_shapes=[
            pltpu.VMEM((feeds + 1, rows, span_y), F32),
            pltpu.VMEM((3, rows, hid, span_y), BF16),
            pltpu.VMEM((3, rows, hid, span_y), BF16),
        ],
        compiler_params=pltpu.CompilerParams(vmem_limit_bytes=16 * 1024 * 1024),
        cost_estimate=pl.CostEstimate(flops=5_000_000_000, bytes_accessed=20_000_000, transcendentals=0),
        name="own_rows",
    )(fields, mask, got_in, got_out, w_first, w_mid, w_last, biases)


def strips(own_low, own_top, got_in, got_out, stress, big, hidden, final, mask, metric):
    span_x, span_y = mask.shape
    hid = hidden.shape[1]
    return pl.pallas_call(
        strip_kernel,
        out_shape=jax.ShapeDtypeStruct((2, span_x, span_y), F32),
        in_specs=[VMEM] * 10,
        out_specs=VMEM,
        scratch_shapes=[
            pltpu.VMEM((own_low.shape[0], STRIP, 2 * span_y), F32),
            pltpu.VMEM((3, STRIP, hid, 2 * span_y), BF16),
            pltpu.VMEM((3, STRIP, hid, 2 * span_y), BF16),
            pltpu.VMEM((3, 2, span_y, span_y), F32),
        ],
        compiler_params=pltpu.CompilerParams(vmem_limit_bytes=8 * 1024 * 1024),
        name="edge_rows",
    )(own_low, own_top, got_in, got_out, stress, big, hidden, final, mask, metric)


def latitude_pairs(count_x, count_y, across):
    at = lambda g, y: g * count_y + y
    pairs = []
    for g in range(count_x):
        for y in range(count_y):
            up = (y % 2 == 0) != across
            if up and y == count_y - 1:
                pairs.append((at(g, y), at(count_x - 1 - g, y)))
            elif up or y > 0:
                pairs.append((at(g, y), at(g, y + 1 if up else y - 1)))
    return pairs


def on_device(fields, ocean_mask, metric, w_first, w_mid, w_last, biases):
    count_x, count_y = lax.axis_size("gx"), lax.axis_size("gy")
    span_x = fields.shape[1]
    inside = [[i, i + 1] for i in range(0, count_x, 2)]
    across = [[i, (i + 1) % count_x] for i in range(1, count_x, 2)]
    both = jnp.concatenate([fields, ocean_mask.astype(BF16)[None]], axis=0)
    edges = jnp.concatenate([both[:, :HALO], both[:, span_x - HALO :]], axis=1)
    got_in = lax.all_gather(edges, "gx", axis_index_groups=inside)
    got_out = lax.all_gather(edges, "gx", axis_index_groups=across)
    pay_in, pay_out, own_low, own_top = pack(fields, ocean_mask, got_in, got_out)
    lat_in = lax.ppermute(pay_in, ("gx", "gy"), latitude_pairs(count_x, count_y, False))
    lat_out = lax.ppermute(pay_out, ("gx", "gy"), latitude_pairs(count_x, count_y, True))
    stress, big, hidden, final = main(fields, ocean_mask, got_in, got_out, w_first, w_mid, w_last, biases)
    return strips(own_low, own_top, lat_in, lat_out, stress, big, hidden, final, ocean_mask, metric)


def solution(mesh):
    placed = (P(None, "gx", "gy"), P("gx", "gy"), P(None, "gy"), P(), P(), P(), P())
    return jax.shard_map(
        on_device, mesh=mesh, in_specs=placed, out_specs=P(None, "gx", "gy"), check_vma=False
    )
```

profile of v0, /device:TPU:56, one launch (start us, length us, event | category | flops | bytes accessed | tf_op | source)
XLA Modules:
  0.0 39.2 jit_solution(673455564593497066)
XLA Ops:
  0.0 0.8 %convert_bitcast_fusion = bf16[1,64,128]{2,1,0:T(8,128)(2,1)S(1)} fusion(s32[64,128]{1,0:T(8,128)} %mask.5), kind=kLoop, calls=%fused_computation.9 | loop fusion | flops 8192 | bytes 49152 | tf_op jit(solution)/shard_map/broadcast_in_dim | solution.py:381
  0.8 0.7 %fusion.5 = bf16[5,16,128]{2,1,0:T(8,128)(2,1)S(1)} fusion(bf16[1,64,128]{2,1,0:T(8,128)(2,1)S(1)} %convert_bitcast_fusion, bf16[4,64,128]{2,1,0:T(8,128)(2,1)} %fields.3), kind=kLoop, calls=%fused_computation.7 | loop fusion | flops 143360 | bytes 102400 | tf_op jit(solution)/shard_map/concatenate | solution.py:382
  1.5 0.0 copy-start.1
  1.5 2.0 %all-gather = bf16[10,16,128]{2,1,0:T(8,128)(2,1)S(1)} all-gather(bf16[5,16,128]{2,1,0:T(8,128)(2,1)S(1)} %fusion.5), channel_id=2, replica_groups={{0,8},{16,24},{32,40},{48,56},{64,72},{80,88},{96,104},{112,120},{128,1..., dimensions={0}, use_global_device_ids=true | all-gather | bytes 61440 | tf_op jit(solution)/shard_map/all_gather | solution.py:383
  3.5 0.0 copy-start
  3.5 16.9 %all-gather.1 = bf16[10,16,128]{2,1,0:T(8,128)(2,1)S(1)} all-gather(bf16[5,16,128]{2,1,0:T(8,128)(2,1)S(1)} %fusion.5), channel_id=3, replica_groups={{8,16},{24,32},{40,48},{56,64},{72,80},{88,96},{104,112},{120,128},{136..., dimensions={0}, use_global_device_ids=true | all-gather | bytes 61440 | tf_op jit(solution)/shard_map/all_gather | solution.py:384
  20.4 0.0 copy-done.1
  20.4 0.0 copy-done
  20.4 0.4 %pack_rows.1 = (bf16[5,8,128]{2,1,0:T(8,128)(2,1)S(1)}, bf16[5,8,128]{2,1,0:T(8,128)(2,1)S(1)}, f32[5,16,128]{2,1,0:T(8,128)S(1)}, f32[5,16,128]{2,1,0:T(8,128)S(1)}) custom-call(bf16[4,64,128]{2,1,0:T(8,128)(2,1)S(1)} %copy-done.1, s32[64,128]{1,0:T(8,128)S(1)} %copy-done, bf16[2,5,16,128]{3,2,1,0:T(8,128)(2,1)S(1)} %bitcast.4, ...), custom_call_target="tpu_custom_call" | custom-call | tf_op jit(solution)/shard_map/pack_rows/pallas_call | solution.py:307
  20.8 3.3 %collective-permute-start = (bf16[5,8,128]{2,1,0:T(8,128)(2,1)S(1)}, bf16[5,8,128]{2,1,0:T(8,128)(2,1)S(1)}, u32[]{:S(2)}, u32[]{:S(2)}) collective-permute-start(bf16[5,8,128]{2,1,0:T(8,128)(2,1)S(1)} %get-tuple-element.15), channel_id=1, source_target_pairs={{0,1},{1,0},{2,3},{3,2},{4,5},{5,4},{6,7},{7,6},{8,9},{9,8},{10,11... | collective-permute-start | bytes 30728 | tf_op jit(solution)/shard_map/ppermute | solution.py:386
  24.1 0.0 copy-start.4
  24.1 0.0 copy-start.5
  24.1 6.7 %collective-permute-start.1 = (bf16[5,8,128]{2,1,0:T(8,128)(2,1)S(1)}, bf16[5,8,128]{2,1,0:T(8,128)(2,1)S(1)}, u32[]{:S(2)}, u32[]{:S(2)}) collective-permute-start(bf16[5,8,128]{2,1,0:T(8,128)(2,1)S(1)} %get-tuple-element.16), channel_id=1, source_target_pairs={{1,2},{2,1},{3,4},{4,3},{5,6},{6,5},{7,767},{9,10},{10,9},{11,12},... | collective-permute-start | bytes 30728 | tf_op jit(solution)/shard_map/ppermute | solution.py:387
  30.8 0.0 copy-done.6
  30.8 0.1 copy.9.w_first
  30.9 0.0 copy-done.3
  31.0 0.0 copy-done.4
  31.0 0.0 copy-done.5
  31.0 4.9 %own_rows.1 = (f32[3,96,128]{2,1,0:T(8,128)S(1)}, bf16[384,176]{1,0:T(8,128)(2,1)S(1)}, bf16[3,48,256]{2,1,0:T(8,128)(2,1)S(1)}, bf16[16,256]{1,0:T(8,128)(2,1)S(1)}) custom-call(bf16[4,64,128]{2,1,0:T(8,128)(2,1)S(1)} %copy-done.1, s32[64,128]{1,0:T(8,128)S(1)} %copy-done, bf16[2,5,16,128]{3,2,1,0:T(8,128)(2,1)S(1)} %bitcast.5, ...), custom_call_target="tpu_custom_call" | custom-call | flops 5000000000 | bytes 20000000 | tf_op jit(solution)/shard_map/own_rows/pallas_call | solution.py:323
  35.8 0.0 collective-permute-done.got_in
  35.8 0.0 collective-permute-done.1.got_out
  35.9 0.0 copy-start.2
  35.9 0.7 %copy-done.2 = f32[2,128]{1,0:T(2,128)S(1)} copy-done((f32[2,128]{1,0:T(2,128)S(1)}, f32[2,128]{1,0:T(2,128)}, u32[]{:S(2)}) %copy-start.2) | copy-done | bytes 1048
  36.5 2.7 %edge_rows.1 = f32[2,64,128]{2,1,0:T(8,128)} custom-call(f32[5,16,128]{2,1,0:T(8,128)S(1)} %get-tuple-element.13.own_low, f32[5,16,128]{2,1,0:T(8,128)S(1)} %get-tuple-element.14.own_top, bf16[5,8,128]{2,1,0:T(8,128)(2,1)S(1)} %collective-permute-done.got_in, bf16[5,8,128]{2,1,0:T(8,128)(2,1)S(1)} %collective-permute-done.1.got_out, ...), custom_call_target="tpu_custom_call" | custom-call | tf_op jit(solution)/shard_map/edge_rows/pallas_call | solution.py:347
  (2 shorter events, 0.0 us)
Async XLA Ops:
  1.5 18.9 %copy-start.1 = (bf16[4,64,128]{2,1,0:T(8,128)(2,1)S(1)}, bf16[4,64,128]{2,1,0:T(8,128)(2,1)}, u32[]{:S(2)}) copy-start(bf16[4,64,128]{2,1,0:T(8,128)(2,1)} %fields.3) | copy-start | bytes 196612
  3.5 16.9 %copy-start = (s32[64,128]{1,0:T(8,128)S(1)}, s32[64,128]{1,0:T(8,128)}, u32[]{:S(2)}) copy-start(s32[64,128]{1,0:T(8,128)} %mask.5) | copy-start | bytes 98308
  3.5 27.5 %copy-start.3 = (bf16[3,5,48,48]{3,2,1,0:T(8,128)(2,1)S(1)}, bf16[3,5,48,48]{3,2,1,0:T(8,128)(2,1)}, u32[]{:S(2)}) copy-start(bf16[3,5,48,48]{3,2,1,0:T(8,128)(2,1)} %w_mid.1) | copy-start | bytes 207364
  20.4 10.4 %copy-start.6 = (bf16[5,48,4]{1,2,0:T(4,128)(2,1)S(1)}, bf16[5,48,4]{1,2,0:T(4,128)(2,1)}, u32[]{:S(2)}) copy-start(bf16[5,48,4]{1,2,0:T(4,128)(2,1)} %param.10) | copy-start | bytes 5764
  20.8 15.0 %collective-permute-start = (bf16[5,8,128]{2,1,0:T(8,128)(2,1)S(1)}, bf16[5,8,128]{2,1,0:T(8,128)(2,1)S(1)}, u32[]{:S(2)}, u32[]{:S(2)}) collective-permute-start(bf16[5,8,128]{2,1,0:T(8,128)(2,1)S(1)} %get-tuple-element.15), channel_id=1, source_target_pairs={{0,1},{1,0},{2,3},{3,2},{4,5},{5,4},{6,7},{7,6},{8,9},{9,8},{10,11... | collective-permute-start | bytes 30728 | tf_op jit(solution)/shard_map/ppermute | solution.py:386
  24.1 6.9 %copy-start.4 = (bf16[5,3,48]{2,1,0:T(4,128)(2,1)S(1)}, bf16[5,3,48]{2,1,0:T(4,128)(2,1)}, u32[]{:S(2)}) copy-start(bf16[5,3,48]{2,1,0:T(4,128)(2,1)} %w_last.1) | copy-start | bytes 4324
  24.1 6.9 %copy-start.5 = (f32[4,48]{1,0:T(4,128)S(1)}, f32[4,48]{1,0:T(4,128)}, u32[]{:S(2)}) copy-start(f32[4,48]{1,0:T(4,128)} %biases.1) | copy-start | bytes 2308
  24.1 11.7 %collective-permute-start.1 = (bf16[5,8,128]{2,1,0:T(8,128)(2,1)S(1)}, bf16[5,8,128]{2,1,0:T(8,128)(2,1)S(1)}, u32[]{:S(2)}, u32[]{:S(2)}) collective-permute-start(bf16[5,8,128]{2,1,0:T(8,128)(2,1)S(1)} %get-tuple-element.16), channel_id=1, source_target_pairs={{1,2},{2,1},{3,4},{4,3},{5,6},{6,5},{7,767},{9,10},{10,9},{11,12},... | collective-permute-start | bytes 30728 | tf_op jit(solution)/shard_map/ppermute | solution.py:387
  35.9 0.7 %copy-start.2 = (f32[2,128]{1,0:T(2,128)S(1)}, f32[2,128]{1,0:T(2,128)}, u32[]{:S(2)}) copy-start(f32[2,128]{1,0:T(2,128)} %metric.1) | copy-start | bytes 3076
where the time goes:
time: 39.6 us; the launch traced here: 39.2 us
  blocking collectives  18.9 us (48%)
  starting transfers between devices  9.93 us (25%)
  Pallas kernels  7.95 us (20%)
  other arithmetic  1.5 us (4%)
  local copies, waits for them, and re-layouts  0.84 us (2%)
    all_gather x1, blocking collectives, on_device(): got_out = lax.all_gather(edges, 'gx', axis_index_groups=across)  16.9 us
    ppermute x1, starting transfers between devices, on_device(): lax.ppermute(pay_out, ('gx', 'gy'), latitude_pairs(count_x, count_y, True))  6.67 us
    pallas_call x1, Pallas kernels, main(): pl.pallas_call(main_kernel, out_shape=[jax.ShapeDtypeStruct((3, rows, spa...  4.86 us
    ppermute x1, starting transfers between devices, on_device(): lax.ppermute(pay_in, ('gx', 'gy'), latitude_pairs(count_x, count_y, False))  3.26 us
    pallas_call x1, Pallas kernels, strips(): pl.pallas_call(strip_kernel, out_shape=jax.ShapeDtypeStruct((2, span_x, s...  2.67 us
    all_gather x1, blocking collectives, on_device(): got_in = lax.all_gather(edges, 'gx', axis_index_groups=inside)  1.95 us
    unnamed x15, local copies, waits for them, and re-layouts  0.84 us
  transfers between devices with their start and end apart: 2, of which 0 were waited for; matrix products, arithmetic and copies ran while one was open for 0% of the time, Pallas kernels for 12%

commit v1 on v0

--- a/solution.py
+++ b/solution.py
@@ -6,7 +6,7 @@
 from jax.sharding import PartitionSpec as P
 
 HALO = 8
-BASE = 2 * HALO
+EARLY = 8
 ONES = 16
 STRIP = 32
 F32 = jnp.float32
@@ -33,6 +33,15 @@
         east.append(jnp.where(odd == 1, far_low, near_low))
         own.append(fields[c].astype(F32) if c < chans - 1 else mask[...].astype(F32))
     return west, own, east
+
+
+def edge_kernel(fields, mask, metric, edges, halved):
+    feeds, span_x, _ = fields.shape
+    for part, start in enumerate((0, span_x - HALO)):
+        rows = slice(part * HALO, (part + 1) * HALO)
+        edges[:feeds, rows] = fields[:, start : start + HALO]
+        edges[feeds, rows] = mask[start : start + HALO]
+    halved[...] = metric[...] * 0.5
 
 
 def pack_kernel(fields, mask, got_in, got_out, pay_in, pay_out, own_low, own_top):
@@ -85,7 +94,7 @@
 def first_taps(window, order):
     pieces = [[] for _ in range(5)]
     for w in window:
-        west, here, east = w[7:15], w[8:16], w[9:17]
+        west, here, east = w[:8], w[1:9], w[2:]
         pieces[0].append(turn(west, 1) + turn(east, -1))
         pieces[1].append(west + east)
         pieces[2].append(turn(west, -1) + turn(east, 1))
@@ -144,15 +153,18 @@
 
 
 def arrange_weights(w_first, w_mid, w_last, biases, big, hidden, final):
-    taps, hid, feeds = w_first.shape
+    taps, feeds, hid = w_first.shape
     n_mid = w_mid.shape[0]
     depth = taps * feeds * 8
     final[...] = jnp.zeros_like(final)
-    spread = jnp.zeros((hid, depth), F32)
+    lanes = 128
+    stacked = [w_first[t].astype(F32) for t in range(taps)]
+    stacked = jnp.concatenate(stacked + [jnp.zeros((lanes - taps * feeds, hid), F32)], axis=0)
+    stacked = jnp.concatenate([stacked, jnp.zeros((lanes, lanes - hid), F32)], axis=1).T
+    a, b = iota((lanes, depth), 0), iota((lanes, depth), 1)
+    place = (b // 8 == a).astype(BF16)
+    spread = jnp.dot(stacked[:hid].astype(BF16), place, preferred_element_type=F32)
     for t in range(taps):
-        a, b = iota((feeds, depth), 0), iota((feeds, depth), 1)
-        place = (b // 8 == t * feeds + a).astype(BF16)
-        spread = spread + jnp.dot(w_first[t], place, preferred_element_type=F32)
         final[: w_last.shape[1], t * hid : (t + 1) * hid] = w_last[t]
         for k in range(n_mid):
             hidden[k, :, t * hid : (t + 1) * hid] = w_mid[k, t]
@@ -165,62 +177,165 @@
         hidden[k, :, taps * hid :] = bias_columns(biases, k + 1).astype(BF16)
 
 
-def main_kernel(
-    fields, mask, got_in, got_out, w_first, w_mid, w_last, biases, stress, big, hidden, final, ext, h_a, h_b
-):
-    chans = fields.shape[0] + 1
-    feeds = chans - 1
-    span_x, span_y = mask.shape
-    n_mid, hid, _ = hidden.shape
+def waits_long():
+    place = lax.rem(lax.axis_index("gx"), lax.axis_size("gx") // 4)
+    top = lax.axis_index("gy") == lax.axis_size("gy") - 1
+    origin = (lax.axis_index("gx") == 0) & (lax.axis_index("gy") == 0)
+    return jnp.logical_not(origin) & ((place == 0) | (top & (place < EARLY)))
+
+
+def halves(v):
+    half = v.shape[1] // 2
+    return v[:, :half], v[:, half:]
+
+
+def masked_stress(summed, ocean_row):
+    return (summed[:8] * ocean_row).astype(BF16).astype(F32)
+
+
+def inner_columns(fields, mask, w_first, w_mid, w_last, biases, stress, kept, big, hidden, final, ext, h_a, h_b):
+    feeds, span_x, span_y = fields.shape
+    n_mid = w_mid.shape[0]
+    hid = w_first.shape[2]
     arrange_weights(w_first, w_mid, w_last, biases, big, hidden, final)
-    west, own, east = sides(fields, mask, got_in, got_out)
-    nothing = jnp.zeros((HALO, span_y), F32)
-    for c in range(chans):
-        ext[c, :HALO] = nothing
-        ext[c, HALO:BASE] = west[c]
-        ext[c, BASE : BASE + span_x] = own[c]
-        ext[c, BASE + span_x : BASE + span_x + HALO] = east[c]
-        ext[c, BASE + span_x + HALO :] = nothing
+    for c in range(feeds):
+        ext[c, :HALO] = jnp.zeros((HALO, span_y), F32)
+        ext[c, HALO : HALO + span_x] = fields[c].astype(F32)
+        ext[c, HALO + span_x :] = jnp.zeros((HALO, span_y), F32)
+    ext[feeds, HALO : HALO + span_x] = mask[...].astype(F32)
 
     def ocean_row(row):
-        return ext[chans - 1, row : row + 1, :]
-
-    def halves(v):
-        return v[:, :span_y], v[:, span_y:]
-
-    for start in range(HALO, BASE + span_x + HALO, 16):
+        return ext[feeds, HALO + row : HALO + row + 1, :]
+
+    def keep(k, row, v):
+        for slot, at in enumerate((k, k + 1, span_x - k - 2, span_x - k - 1)):
+            if row == at:
+                kept[k - 1, slot] = v
+
+    for start in range(0, span_x, 16):
         taps = [
-            first_taps([ext[c, row - 8 : row + 16, :] for c in range(feeds)], ALONG_X)
+            first_taps([ext[c, HALO + row - 1 : HALO + row + 9, :] for c in range(feeds)], ALONG_X)
             for row in (start, start + 8)
         ]
         summed = jnp.dot(big[...], jnp.concatenate(taps, axis=1), preferred_element_type=F32)
         for part, row in zip(halves(summed), (start, start + 8)):
             for r in range(8):
-                put(h_a, row + r, activate(part[r * hid : (r + 1) * hid], ocean_row(row + r)))
-
-    def layer(weights, src, reach, finish):
+                v = activate(part[r * hid : (r + 1) * hid], ocean_row(row + r))
+                put(h_a, row + r, v)
+                keep(1, row + r, v)
+
+    def layer(weights, src, k, finish):
         cached = loader(src)
-        for start in range(BASE - reach, BASE + span_x + reach, 2):
+        for start in range(k, span_x - k, 2):
             taps = [hidden_taps(cached, row, ALONG_X) for row in (start, start + 1)]
             summed = jnp.dot(weights, jnp.concatenate(taps, axis=1), preferred_element_type=F32)
             for part, row in zip(halves(summed), (start, start + 1)):
                 finish(part, row)
 
     src, dst = h_a, h_b
-    for k in range(n_mid):
-        layer(hidden[k], src, n_mid + 1 - k, lambda v, row: put(dst, row, activate(v, ocean_row(row))))
+    for k in range(2, n_mid + 2):
+
+        def finish(summed, row):
+            v = activate(summed, ocean_row(row))
+            put(dst, row, v)
+            keep(k, row, v)
+
+        layer(hidden[k - 2], src, k, finish)
         src, dst = dst, src
 
     def finish(summed, row):
-        v = (summed[:8] * ocean_row(row)).astype(BF16).astype(F32)
+        v = masked_stress(summed, ocean_row(row))
         for c in range(3):
-            stress[c, row : row + 1, :] = v[c : c + 1]
-
-    layer(final[...], src, 1, finish)
+            stress[c, HALO + row : HALO + row + 1, :] = v[c : c + 1]
+
+    layer(final[...], src, n_mid + 2, finish)
+
+
+def early_kernel(
+    edges, got_in, fields, mask, w_first, w_mid, w_last, biases,
+    edges_out, stress, kept, big, hidden, final, ext, h_a, h_b,
+):
+    del got_in
+    edges_out[...] = edges[...]
+
+    @pl.when(waits_long())
+    def _():
+        inner_columns(
+            fields, mask, w_first, w_mid, w_last, biases, stress, kept, big, hidden, final, ext, h_a, h_b
+        )
+
+
+def side_kernel(
+    fields, mask, got_in, got_out, w_first, w_mid, w_last, biases, stress_in, kept_in, big_in, hidden_in, final_in,
+    stress, big, hidden, final, ext, h_a, h_b, rows_a, rows_b, kept,
+):
+    feeds, span_x, span_y = fields.shape
+    n_mid = w_mid.shape[0]
+    hid = w_first.shape[2]
+
+    @pl.when(waits_long())
+    def _():
+        for done, here in ((stress_in, stress), (kept_in, kept), (big_in, big), (hidden_in, hidden), (final_in, final)):
+            here[...] = done[...]
+
+    @pl.when(jnp.logical_not(waits_long()))
+    def _():
+        inner_columns(
+            fields, mask, w_first, w_mid, w_last, biases, stress, kept, big, hidden, final, ext, h_a, h_b
+        )
+
+    west, own, east = sides(fields, mask, got_in, got_out)
+    for c in range(feeds + 1):
+        ext[c, :HALO] = west[c]
+        ext[c, HALO : HALO + span_x] = own[c]
+        ext[c, HALO + span_x :] = east[c]
+
+    def places(k, slot):
+        return k - 8 + slot, span_x - 2 - k + slot
+
+    def ocean_row(row):
+        return ext[feeds, HALO + row : HALO + row + 1, :]
+
+    def fill(dst, k):
+        for slot in range(2):
+            put(dst.at[0], 8 + slot, kept[k - 1, slot])
+            put(dst.at[1], slot, kept[k - 1, 2 + slot])
+
+    starts = (-6, span_x - 2)
+    taps = [
+        first_taps([ext[c, HALO + row - 1 : HALO + row + 9, :] for c in range(feeds)], ALONG_X)
+        for row in starts
+    ]
+    summed = jnp.dot(big[...], jnp.concatenate(taps, axis=1), preferred_element_type=F32)
+    for side, part in enumerate(halves(summed)):
+        for slot in range(2, 8):
+            row = places(1, slot)[side]
+            r = row - starts[side]
+            put(rows_a.at[side], slot, activate(part[r * hid : (r + 1) * hid], ocean_row(row)))
+    fill(rows_a, 1)
+
+    src, dst = rows_a, rows_b
+    for k in range(2, n_mid + 3):
+        loads = [loader(src.at[side]) for side in range(2)]
+        weights = hidden[k - 2] if k < n_mid + 2 else final[...]
+        for slot in range(2, 8):
+            taps = [hidden_taps(loads[0], slot + 1, ALONG_X), hidden_taps(loads[1], slot - 1, ALONG_X)]
+            summed = jnp.dot(weights, jnp.concatenate(taps, axis=1), preferred_element_type=F32)
+            for side, part in enumerate(halves(summed)):
+                row = places(k, slot)[side]
+                if k < n_mid + 2:
+                    put(dst.at[side], slot, activate(part, ocean_row(row)))
+                else:
+                    v = masked_stress(part, ocean_row(row))
+                    for c in range(3):
+                        stress[c, HALO + row : HALO + row + 1, :] = v[c : c + 1]
+        if k < n_mid + 2:
+            fill(dst, k)
+        src, dst = dst, src
 
 
 def strip_kernel(
-    own_low, own_top, got_in, got_out, stress, big, hidden, final, mask, metric, out, ext, h_a, h_b, edge
+    own_low, own_top, got_in, got_out, stress, big, hidden, final, mask, halved, out, ext, h_a, h_b, edge
 ):
     chans = own_low.shape[0]
     feeds = chans - 1
@@ -250,7 +365,7 @@
 
     for row in (8, 16):
         taps = [
-            first_taps([ext[c, row - 8 : row + 16, half * span_y : (half + 1) * span_y] for c in range(feeds)], ALONG_Y)
+            first_taps([ext[c, row - 1 : row + 9, half * span_y : (half + 1) * span_y] for c in range(feeds)], ALONG_Y)
             for half in range(2)
         ]
         summed = jnp.dot(big[...], jnp.concatenate(taps, axis=1), preferred_element_type=F32)
@@ -265,32 +380,32 @@
             summed = jnp.dot(hidden[k], taps, preferred_element_type=F32)
             put_both(dst, row, activate(summed, ocean_row(row)))
         src, dst = dst, src
-    edge[...] = jnp.zeros_like(edge)
+    slot = 2 * HALO
     cached = loader(src)
     for row in range(13, 19):
         summed = jnp.dot(final[...], hidden_taps(cached, row, ALONG_Y), preferred_element_type=F32)
-        v = (summed[:8] * ocean_row(row)).astype(BF16).astype(F32)
-        low, high = row - 14, span_y - 18 + row
+        v = masked_stress(summed, ocean_row(row))
         for c in range(3):
-            for lat, part in ((low, v[c : c + 1, :span_y]), (high, v[c : c + 1, span_y:])):
-                tile, slot = (0, lat) if 0 <= lat < span_y else (1, lat % span_y)
-                edge[c, tile, slot : slot + 1, :] = part
-
-    half_x = metric[0:1, :] * 0.5
-    half_y = metric[1:2, :] * 0.5
+            edge[c * slot + row - 13 : c * slot + row - 12, :] = v[c : c + 1, :span_y]
+            edge[c * slot + row - 5 : c * slot + row - 4, :] = v[c : c + 1, span_y:]
+    turned = edge[...].T[HALO - 1 : HALO + span_x + 1]
+
+    half_x = halved[0:1, :]
+    half_y = halved[1:2, :]
     ocean = mask[...].astype(F32)
     lane = iota((span_x + 2, span_y), 1)
+    inner = lane[:span_x]
     planes, north, south = [], [], []
     for c in range(3):
-        inside = edge[c, 0].T[HALO - 1 : HALO + span_x + 1]
-        beyond = edge[c, 1].T[HALO : HALO + span_x]
-        near = (lane < 5) | (lane >= span_y - 5)
-        plane = jnp.where(near, inside, stress[c, BASE - 1 : BASE + span_x + 1, :])
+        low = turn(turned, -(c * slot + 1))
+        high = turn(turned, span_y - 5 - (c * slot + HALO))
+        plane = jnp.where(lane < 5, low, jnp.where(lane >= span_y - 5, high, stress[c, HALO - 1 : HALO + span_x + 1, :]))
         here = plane[1 : 1 + span_x]
-        inner = lane[:span_x]
+        beyond = turn(turned[1 : 1 + span_x], span_y - 1 - (c * slot + HALO + 5))
+        below = turn(turned[1 : 1 + span_x], -c * slot)
         planes.append(plane)
-        north.append(turn(jnp.where(inner == 0, beyond, here), -1))
-        south.append(turn(jnp.where(inner == span_y - 1, beyond, here), 1))
+        north.append(jnp.where(inner == span_y - 1, beyond, turn(here, -1)))
+        south.append(jnp.where(inner == 0, below, turn(here, 1)))
 
     def diff_x(c):
         return (planes[c][2:] - planes[c][:span_x]) * half_x
@@ -315,33 +430,72 @@
     )(fields, mask, got_in, got_out)
 
 
-def main(fields, mask, got_in, got_out, w_first, w_mid, w_last, biases):
-    span_x, span_y = mask.shape
-    rows = span_x + 4 * HALO
-    taps, hid, feeds = w_first.shape
+def outermost(fields, mask, metric):
+    return pl.pallas_call(
+        edge_kernel,
+        out_shape=[
+            jax.ShapeDtypeStruct((fields.shape[0] + 1, 2 * HALO, fields.shape[2]), BF16),
+            jax.ShapeDtypeStruct(metric.shape, F32),
+        ],
+        in_specs=[VMEM] * 3,
+        out_specs=[VMEM] * 2,
+        compiler_params=pltpu.CompilerParams(vmem_limit_bytes=4 * 1024 * 1024),
+        cost_estimate=pl.CostEstimate(flops=10_000_000_000, bytes_accessed=1_000_000, transcendentals=0),
+        name="outermost_columns",
+    )(fields, mask, metric)
+
+
+def inner_shapes(fields, w_first, w_mid):
+    feeds, span_x, span_y = fields.shape
+    taps, _, hid = w_first.shape
     n_mid = w_mid.shape[0]
+    rows = span_x + 2 * HALO
+    outs = [
+        jax.ShapeDtypeStruct((3, rows, span_y), F32),
+        jax.ShapeDtypeStruct((n_mid + 1, 4, hid, span_y), BF16),
+        jax.ShapeDtypeStruct((8 * hid, taps * feeds * 8 + ONES), BF16),
+        jax.ShapeDtypeStruct((n_mid, hid, taps * hid + ONES), BF16),
+        jax.ShapeDtypeStruct((16, taps * hid + ONES), BF16),
+    ]
+    scratch = [
+        pltpu.VMEM((feeds + 1, rows, span_y), F32),
+        pltpu.VMEM((3, span_x, hid, span_y), BF16),
+        pltpu.VMEM((3, span_x, hid, span_y), BF16),
+    ]
+    return outs, scratch
+
+
+def early(edges, got_in, fields, mask, w_first, w_mid, w_last, biases):
+    outs, scratch = inner_shapes(fields, w_first, w_mid)
     return pl.pallas_call(
-        main_kernel,
-        out_shape=[
-            jax.ShapeDtypeStruct((3, rows, span_y), F32),
-            jax.ShapeDtypeStruct((8 * hid, taps * feeds * 8 + ONES), BF16),
-            jax.ShapeDtypeStruct((n_mid, hid, taps * hid + ONES), BF16),
-            jax.ShapeDtypeStruct((16, taps * hid + ONES), BF16),
-        ],
+        early_kernel,
+        out_shape=[jax.ShapeDtypeStruct(edges.shape, edges.dtype)] + outs,
         in_specs=[VMEM] * 8,
+        out_specs=[VMEM] * 6,
+        scratch_shapes=scratch,
+        compiler_params=pltpu.CompilerParams(vmem_limit_bytes=12 * 1024 * 1024),
+        name="inner_early",
+    )(edges, got_in, fields, mask, w_first, w_mid, w_last, biases)
+
+
+def side_columns(fields, mask, got_in, got_out, w_first, w_mid, w_last, biases, done):
+    outs, scratch = inner_shapes(fields, w_first, w_mid)
+    hid, span_y = w_first.shape[2], mask.shape[1]
+    return pl.pallas_call(
+        side_kernel,
+        out_shape=outs[:1] + outs[2:],
+        in_specs=[VMEM] * 13,
         out_specs=[VMEM] * 4,
-        scratch_shapes=[
-            pltpu.VMEM((feeds + 1, rows, span_y), F32),
-            pltpu.VMEM((3, rows, hid, span_y), BF16),
-            pltpu.VMEM((3, rows, hid, span_y), BF16),
-        ],
-        compiler_params=pltpu.CompilerParams(vmem_limit_bytes=16 * 1024 * 1024),
+        scratch_shapes=scratch
+        + [pltpu.VMEM((2, 3, 10, hid, span_y), BF16)] * 2
+        + [pltpu.VMEM(outs[1].shape, BF16)],
+        compiler_params=pltpu.CompilerParams(vmem_limit_bytes=12 * 1024 * 1024),
         cost_estimate=pl.CostEstimate(flops=5_000_000_000, bytes_accessed=20_000_000, transcendentals=0),
-        name="own_rows",
-    )(fields, mask, got_in, got_out, w_first, w_mid, w_last, biases)
-
-
-def strips(own_low, own_top, got_in, got_out, stress, big, hidden, final, mask, metric):
+        name="inner_and_sides",
+    )(fields, mask, got_in, got_out, w_first, w_mid, w_last, biases, *done)
+
+
+def strips(own_low, own_top, got_in, got_out, stress, big, hidden, final, mask, halved):
     span_x, span_y = mask.shape
     hid = hidden.shape[1]
     return pl.pallas_call(
@@ -353,11 +507,11 @@
             pltpu.VMEM((own_low.shape[0], STRIP, 2 * span_y), F32),
             pltpu.VMEM((3, STRIP, hid, 2 * span_y), BF16),
             pltpu.VMEM((3, STRIP, hid, 2 * span_y), BF16),
-            pltpu.VMEM((3, 2, span_y, span_y), F32),
+            pltpu.VMEM((span_y, span_y), F32),
         ],
         compiler_params=pltpu.CompilerParams(vmem_limit_bytes=8 * 1024 * 1024),
         name="edge_rows",
-    )(own_low, own_top, got_in, got_out, stress, big, hidden, final, mask, metric)
+    )(own_low, own_top, got_in, got_out, stress, big, hidden, final, mask, halved)
 
 
 def latitude_pairs(count_x, count_y, across):
@@ -375,18 +529,19 @@
 
 def on_device(fields, ocean_mask, metric, w_first, w_mid, w_last, biases):
     count_x, count_y = lax.axis_size("gx"), lax.axis_size("gy")
-    span_x = fields.shape[1]
     inside = [[i, i + 1] for i in range(0, count_x, 2)]
     across = [[i, (i + 1) % count_x] for i in range(1, count_x, 2)]
-    both = jnp.concatenate([fields, ocean_mask.astype(BF16)[None]], axis=0)
-    edges = jnp.concatenate([both[:, :HALO], both[:, span_x - HALO :]], axis=1)
+    weights = (jnp.swapaxes(w_first, 1, 2), w_mid, w_last, biases)
+    ocean_mask = ocean_mask.astype(BF16)
+    edges, halved = outermost(fields, ocean_mask, metric)
     got_in = lax.all_gather(edges, "gx", axis_index_groups=inside)
+    edges, *done = early(edges, got_in, fields, ocean_mask, *weights)
     got_out = lax.all_gather(edges, "gx", axis_index_groups=across)
     pay_in, pay_out, own_low, own_top = pack(fields, ocean_mask, got_in, got_out)
     lat_in = lax.ppermute(pay_in, ("gx", "gy"), latitude_pairs(count_x, count_y, False))
     lat_out = lax.ppermute(pay_out, ("gx", "gy"), latitude_pairs(count_x, count_y, True))
-    stress, big, hidden, final = main(fields, ocean_mask, got_in, got_out, w_first, w_mid, w_last, biases)
-    return strips(own_low, own_top, lat_in, lat_out, stress, big, hidden, final, ocean_mask, metric)
+    stress, big, hidden, final = side_columns(fields, ocean_mask, got_in, got_out, *weights, done)
+    return strips(own_low, own_top, lat_in, lat_out, stress, big, hidden, final, ocean_mask, halved)
 
 
 def solution(mesh):

time: 39.6 us -> 35.5 us (0.90)
  blocking collectives: 18.9 us -> 14.8 us
  Pallas kernels: 7.95 us -> 8.79 us
  other arithmetic: 1.5 us -> 0.78 us
    all_gather x1, blocking collectives: 16.9 us -> 12.8 us  [on_device(): got_out = lax.all_gather(edges, 'gx', axis_index_groups=across)]
    pallas_call x1 -> x3, Pallas kernels: 4.86 us -> 5.65 us  [the longest x1 4 us: early(): pl.pallas_call(early_kernel, out_shape=[jax.ShapeDtypeStruct(edges.shape,...]
    convert_element_type x0 -> x1, other arithmetic: none -> 0.78 us  [on_device(): ocean_mask = ocean_mask.astype(BF16)]
    broadcast_in_dim x1 -> x0, other arithmetic: 0.76 us -> none  [on_device(): both = jnp.concatenate([fields, ocean_mask.astype(BF16)[None]], axis=0)]
    concatenate x1 -> x0, other arithmetic: 0.74 us -> none  [on_device(): edges = jnp.concatenate([both[:, :HALO], both[:, span_x - HALO:]], axis=1)]
    unnamed x15 -> x14, local copies, waits for them, and re-layouts: 0.84 us -> 0.86 us
  transfers between devices with their start and end apart: 2 -> 2, of which waited for: 0 -> 0; matrix products, arithmetic and copies ran while one was open for 0% -> 0% of each run, Pallas kernels for 12% -> 5%
where the time goes in v1:
time: 35.5 us; the launch traced here: 35.3 us
  blocking collectives  14.8 us (42%)
  starting transfers between devices  9.93 us (28%)
  Pallas kernels  8.79 us (25%)
  local copies, waits for them, and re-layouts  0.86 us (2%)
  other arithmetic  0.78 us (2%)
    all_gather x1, blocking collectives, on_device(): got_out = lax.all_gather(edges, 'gx', axis_index_groups=across)  12.8 us
    ppermute x1, starting transfers between devices, on_device(): lax.ppermute(pay_out, ('gx', 'gy'), latitude_pairs(count_x, count_y, True))  6.67 us
    pallas_call x1, Pallas kernels, early(): pl.pallas_call(early_kernel, out_shape=[jax.ShapeDtypeStruct(edges.shape,...  4 us
    ppermute x1, starting transfers between devices, on_device(): lax.ppermute(pay_in, ('gx', 'gy'), latitude_pairs(count_x, count_y, False))  3.26 us
    pallas_call x1, Pallas kernels, strips(): pl.pallas_call(strip_kernel, out_shape=jax.ShapeDtypeStruct((2, span_x, s...  2.72 us
    all_gather x1, blocking collectives, on_device(): got_in = lax.all_gather(edges, 'gx', axis_index_groups=inside)  1.97 us
    pallas_call x1, Pallas kernels, side_columns(): pl.pallas_call(side_kernel, out_shape=outs[:1] + outs[2:], in_specs=[VMEM...  1.64 us
    unnamed x14, local copies, waits for them, and re-layouts  0.86 us
  transfers between devices with their start and end apart: 2, of which 0 were waited for; matrix products, arithmetic and copies ran while one was open for 0% of the time, Pallas kernels for 5%

profile of v1, /device:TPU:56, one launch (start us, length us, event | category | flops | bytes accessed | tf_op | source)
XLA Modules:
  0.0 35.3 jit_solution(4140236641142111196)
XLA Ops:
  0.0 0.0 copy-start.6
  0.0 0.8 %convert_element_type.3.mask = bf16[64,128]{1,0:T(8,128)(2,1)S(1)} convert(s32[64,128]{1,0:T(8,128)} %param.8) | non-fusion elementwise | flops 8192 | bytes 49152 | tf_op jit(solution)/shard_map/convert_element_type | solution.py:535
  0.8 0.0 copy-done.6
  0.8 0.0 copy-start
  0.8 0.8 %copy-done = bf16[4,64,128]{2,1,0:T(8,128)(2,1)S(1)} copy-done((bf16[4,64,128]{2,1,0:T(8,128)(2,1)S(1)}, bf16[4,64,128]{2,1,0:T(8,128)(2,1)}, u32[]{:S(2)}) %copy-start) | copy-done | bytes 65560
  1.6 0.0 copy-start.2
  1.6 0.0 copy-start.3
  1.6 0.0 copy-start.4
  1.6 0.0 copy-start.1
  1.7 2.0 %all-gather = bf16[10,16,128]{2,1,0:T(8,128)(2,1)S(1)} all-gather(bf16[5,16,128]{2,1,0:T(8,128)(2,1)S(1)} %get-tuple-element.21.edges), channel_id=2, replica_groups={{0,8},{16,24},{32,40},{48,56},{64,72},{80,88},{96,104},{112,120},{128,1..., dimensions={0}, use_global_device_ids=true | all-gather | bytes 61440 | tf_op jit(solution)/shard_map/all_gather | solution.py:537
  3.6 0.0 copy-done.2
  3.6 0.0 copy-done.3
  3.6 0.0 copy-done.4
  3.6 0.0 copy-done.5
  3.6 0.0 copy-done.1
  3.7 4.0 %inner_early.1 = (bf16[5,16,128]{2,1,0:T(8,128)(2,1)S(1)}, f32[3,80,128]{2,1,0:T(8,128)S(1)}, bf16[4,4,48,128]{3,2,1,0:T(8,128)(2,1)S(1)}, bf16[384,176]{1,0:T(8...) custom-call(bf16[5,16,128]{2,1,0:T(8,128)(2,1)S(1)} %get-tuple-element.21.edges, ...), custom_call_target="tpu_custom_call" | custom-call | tf_op jit(solution)/shard_map/inner_early/pallas_call | solution.py:470
  7.7 12.8 %all-gather.1 = bf16[10,16,128]{2,1,0:T(8,128)(2,1)S(1)} all-gather(bf16[5,16,128]{2,1,0:T(8,128)(2,1)S(1)} %get-tuple-element.22), channel_id=3, replica_groups={{8,16},{24,32},{40,48},{56,64},{72,80},{88,96},{104,112},{120,128},{136..., dimensions={0}, use_global_device_ids=true | all-gather | bytes 61440 | tf_op jit(solution)/shard_map/all_gather | solution.py:539
  20.5 0.4 %pack_rows.1 = (bf16[5,8,128]{2,1,0:T(8,128)(2,1)S(1)}, bf16[5,8,128]{2,1,0:T(8,128)(2,1)S(1)}, f32[5,16,128]{2,1,0:T(8,128)S(1)}, f32[5,16,128]{2,1,0:T(8,128)S(1)}) custom-call(bf16[4,64,128]{2,1,0:T(8,128)(2,1)S(1)} %copy-done.1, bf16[64,128]{1,0:T(8,128)(2,1)S(1)} %convert_element_type.3.mask, bf16[2,5,16,128]{3,2,1,0:T(8,128)(2,1)S(1)} %bitcast.4, ...), custom_call_target="tpu_custom_call" | custom-call | tf_op jit(solution)/shard_map/pack_rows/pallas_call | solution.py:422
  20.9 3.3 %collective-permute-start = (bf16[5,8,128]{2,1,0:T(8,128)(2,1)S(1)}, bf16[5,8,128]{2,1,0:T(8,128)(2,1)S(1)}, u32[]{:S(2)}, u32[]{:S(2)}) collective-permute-start(bf16[5,8,128]{2,1,0:T(8,128)(2,1)S(1)} %get-tuple-element.25), channel_id=1, source_target_pairs={{0,1},{1,0},{2,3},{3,2},{4,5},{5,4},{6,7},{7,6},{8,9},{9,8},{10,11... | collective-permute-start | bytes 30728 | tf_op jit(solution)/shard_map/ppermute | solution.py:541
  24.2 6.7 %collective-permute-start.1 = (bf16[5,8,128]{2,1,0:T(8,128)(2,1)S(1)}, bf16[5,8,128]{2,1,0:T(8,128)(2,1)S(1)}, u32[]{:S(2)}, u32[]{:S(2)}) collective-permute-start(bf16[5,8,128]{2,1,0:T(8,128)(2,1)S(1)} %get-tuple-element.26), channel_id=1, source_target_pairs={{1,2},{2,1},{3,4},{4,3},{5,6},{6,5},{7,767},{9,10},{10,9},{11,12},... | collective-permute-start | bytes 30728 | tf_op jit(solution)/shard_map/ppermute | solution.py:542
  30.9 1.6 %inner_and_sides.1 = (f32[3,80,128]{2,1,0:T(8,128)S(1)}, bf16[384,176]{1,0:T(8,128)(2,1)S(1)}, bf16[3,48,256]{2,1,0:T(8,128)(2,1)S(1)}, bf16[16,256]{1,0:T(8,128)(2,1)S(1)}) custom-call(bf16[4,64,128]{2,1,0:T(8,128)(2,1)S(1)} %copy-done.1, bf16[64,128]{1,0:T(8,128)(2,1)S(1)} %convert_element_type.3.mask, bf16[2,5,16,128]{3,2,1,0:T(8,128)(2,1)S(1)} %bitcast.5, ...), custom_call_target="tpu_custom_call" | custom-call | flops 5000000000 | bytes 20000000 | tf_op jit(solution)/shard_map/inner_and_sides/pallas_call | solution.py:484
  32.5 0.0 collective-permute-done.got_in
  32.5 0.0 collective-permute-done.1.got_out
  32.5 2.7 %edge_rows.1 = f32[2,64,128]{2,1,0:T(8,128)} custom-call(f32[5,16,128]{2,1,0:T(8,128)S(1)} %get-tuple-element.23.own_low, f32[5,16,128]{2,1,0:T(8,128)S(1)} %get-tuple-element.24.own_top, bf16[5,8,128]{2,1,0:T(8,128)(2,1)S(1)} %collective-permute-done.got_in, bf16[5,8,128]{2,1,0:T(8,128)(2,1)S(1)} %collective-permute-done.1.got_out, ...), custom_call_target="tpu_custom_call" | custom-call | tf_op jit(solution)/shard_map/edge_rows/pallas_call | solution.py:501
  (2 shorter events, 0.0 us)
Async XLA Ops:
  0.0 0.8 %copy-start.6 = (f32[2,128]{1,0:T(2,128)S(1)}, f32[2,128]{1,0:T(2,128)}, u32[]{:S(2)}) copy-start(f32[2,128]{1,0:T(2,128)} %metric.1) | copy-start | bytes 3076
  0.8 0.8 %copy-start = (bf16[4,64,128]{2,1,0:T(8,128)(2,1)S(1)}, bf16[4,64,128]{2,1,0:T(8,128)(2,1)}, u32[]{:S(2)}) copy-start(bf16[4,64,128]{2,1,0:T(8,128)(2,1)} %fields.7) | copy-start | bytes 196612
  1.6 2.0 %copy-start.2 = (bf16[3,5,48,48]{3,2,1,0:T(8,128)(2,1)S(1)}, bf16[3,5,48,48]{3,2,1,0:T(8,128)(2,1)}, u32[]{:S(2)}) copy-start(bf16[3,5,48,48]{3,2,1,0:T(8,128)(2,1)} %w_mid.3) | copy-start | bytes 207364
  1.6 2.0 %copy-start.3 = (bf16[5,48,4]{1,2,0:T(4,128)(2,1)S(1)}, bf16[5,48,4]{1,2,0:T(4,128)(2,1)}, u32[]{:S(2)}) copy-start(bf16[5,48,4]{1,2,0:T(4,128)(2,1)} %param.10) | copy-start | bytes 5764
  1.6 2.0 %copy-start.4 = (bf16[5,3,48]{2,1,0:T(4,128)(2,1)S(1)}, bf16[5,3,48]{2,1,0:T(4,128)(2,1)}, u32[]{:S(2)}) copy-start(bf16[5,3,48]{2,1,0:T(4,128)(2,1)} %w_last.3) | copy-start | bytes 4324
  1.6 2.0 %copy-start.5 = (f32[4,48]{1,0:T(4,128)S(1)}, f32[4,48]{1,0:T(4,128)}, u32[]{:S(2)}) copy-start(f32[4,48]{1,0:T(4,128)} %biases.3) | copy-start | bytes 2308
  1.6 2.0 %copy-start.1 = (bf16[4,64,128]{2,1,0:T(8,128)(2,1)S(1)}, bf16[4,64,128]{2,1,0:T(8,128)(2,1)}, u32[]{:S(2)}) copy-start(bf16[4,64,128]{2,1,0:T(8,128)(2,1)} %fields.7) | copy-start | bytes 196612
  20.9 11.6 %collective-permute-start = (bf16[5,8,128]{2,1,0:T(8,128)(2,1)S(1)}, bf16[5,8,128]{2,1,0:T(8,128)(2,1)S(1)}, u32[]{:S(2)}, u32[]{:S(2)}) collective-permute-start(bf16[5,8,128]{2,1,0:T(8,128)(2,1)S(1)} %get-tuple-element.25), channel_id=1, source_target_pairs={{0,1},{1,0},{2,3},{3,2},{4,5},{5,4},{6,7},{7,6},{8,9},{9,8},{10,11... | collective-permute-start | bytes 30728 | tf_op jit(solution)/shard_map/ppermute | solution.py:541
  24.2 8.3 %collective-permute-start.1 = (bf16[5,8,128]{2,1,0:T(8,128)(2,1)S(1)}, bf16[5,8,128]{2,1,0:T(8,128)(2,1)S(1)}, u32[]{:S(2)}, u32[]{:S(2)}) collective-permute-start(bf16[5,8,128]{2,1,0:T(8,128)(2,1)S(1)} %get-tuple-element.26), channel_id=1, source_target_pairs={{1,2},{2,1},{3,4},{4,3},{5,6},{6,5},{7,767},{9,10},{10,9},{11,12},... | collective-permute-start | bytes 30728 | tf_op jit(solution)/shard_map/ppermute | solution.py:542

commit v2 on v1

--- a/solution.py
+++ b/solution.py
@@ -35,12 +35,12 @@
     return west, own, east
 
 
-def edge_kernel(fields, mask, metric, edges, halved):
-    feeds, span_x, _ = fields.shape
+def edge_kernel(columns, mask, metric, edges, halved):
+    feeds = columns.shape[0]
+    span_x = mask.shape[0]
+    edges[:feeds] = columns[...]
     for part, start in enumerate((0, span_x - HALO)):
-        rows = slice(part * HALO, (part + 1) * HALO)
-        edges[:feeds, rows] = fields[:, start : start + HALO]
-        edges[feeds, rows] = mask[start : start + HALO]
+        edges[feeds, part * HALO : (part + 1) * HALO] = mask[start : start + HALO].astype(F32).astype(BF16)
     halved[...] = metric[...] * 0.5
 
 
@@ -265,17 +265,16 @@
         )
 
 
-def side_kernel(
-    fields, mask, got_in, got_out, w_first, w_mid, w_last, biases, stress_in, kept_in, big_in, hidden_in, final_in,
-    stress, big, hidden, final, ext, h_a, h_b, rows_a, rows_b, kept,
+def late_kernel(
+    fields, mask, w_first, w_mid, w_last, biases, stress_in, kept_in, big_in, hidden_in, final_in, lat_out,
+    stress, kept, big, hidden, final, ext, h_a, h_b,
 ):
-    feeds, span_x, span_y = fields.shape
-    n_mid = w_mid.shape[0]
-    hid = w_first.shape[2]
+    del lat_out
 
     @pl.when(waits_long())
     def _():
-        for done, here in ((stress_in, stress), (kept_in, kept), (big_in, big), (hidden_in, hidden), (final_in, final)):
+        pairs = ((stress_in, stress), (kept_in, kept), (big_in, big), (hidden_in, hidden), (final_in, final))
+        for done, here in pairs:
             here[...] = done[...]
 
     @pl.when(jnp.logical_not(waits_long()))
@@ -284,11 +283,11 @@
             fields, mask, w_first, w_mid, w_last, biases, stress, kept, big, hidden, final, ext, h_a, h_b
         )
 
-    west, own, east = sides(fields, mask, got_in, got_out)
-    for c in range(feeds + 1):
-        ext[c, :HALO] = west[c]
-        ext[c, HALO : HALO + span_x] = own[c]
-        ext[c, HALO + span_x :] = east[c]
+
+def side_layers(ext, kept, span_x, big, hidden, final, src, dst, stress):
+    n_mid, hid, _ = hidden.shape
+    feeds = ext.shape[0] - 1
+    starts = (-6, span_x - 2)
 
     def places(k, slot):
         return k - 8 + slot, span_x - 2 - k + slot
@@ -301,20 +300,17 @@
             put(dst.at[0], 8 + slot, kept[k - 1, slot])
             put(dst.at[1], slot, kept[k - 1, 2 + slot])
 
-    starts = (-6, span_x - 2)
     taps = [
-        first_taps([ext[c, HALO + row - 1 : HALO + row + 9, :] for c in range(feeds)], ALONG_X)
-        for row in starts
+        first_taps([ext[c, HALO + row - 1 : HALO + row + 9, :] for c in range(feeds)], ALONG_X) for row in starts
     ]
     summed = jnp.dot(big[...], jnp.concatenate(taps, axis=1), preferred_element_type=F32)
     for side, part in enumerate(halves(summed)):
         for slot in range(2, 8):
             row = places(1, slot)[side]
             r = row - starts[side]
-            put(rows_a.at[side], slot, activate(part[r * hid : (r + 1) * hid], ocean_row(row)))
-    fill(rows_a, 1)
-
-    src, dst = rows_a, rows_b
+            put(src.at[side], slot, activate(part[r * hid : (r + 1) * hid], ocean_row(row)))
+    fill(src, 1)
+    yield
     for k in range(2, n_mid + 3):
         loads = [loader(src.at[side]) for side in range(2)]
         weights = hidden[k - 2] if k < n_mid + 2 else final[...]
@@ -329,31 +325,18 @@
                     v = masked_stress(part, ocean_row(row))
                     for c in range(3):
                         stress[c, HALO + row : HALO + row + 1, :] = v[c : c + 1]
+            yield
         if k < n_mid + 2:
             fill(dst, k)
         src, dst = dst, src
 
 
-def strip_kernel(
-    own_low, own_top, got_in, got_out, stress, big, hidden, final, mask, halved, out, ext, h_a, h_b, edge
-):
-    chans = own_low.shape[0]
-    feeds = chans - 1
-    span_x, span_y = mask.shape
+def strip_layers(ext, span_y, big, hidden, final, src, dst, edge):
     n_mid, hid, _ = hidden.shape
-    odd = lax.rem(lax.axis_index("gy"), 2) == 1
-    ext[...] = jnp.zeros_like(ext)
-    for c in range(chans):
-        inner, outer = got_in[c].astype(F32), got_out[c].astype(F32)
-        below = jnp.where(odd, inner, outer)
-        above = jnp.where(odd, outer, inner)
-        ext[c, 6:14, :span_y] = below
-        ext[c, 14:30, :span_y] = own_low[c]
-        ext[c, 2:18, span_y:] = own_top[c]
-        ext[c, 18:26, span_y:] = above
+    feeds = ext.shape[0] - 1
 
     def ocean_row(row):
-        return ext[chans - 1, row : row + 1, :]
+        return ext[feeds, row : row + 1, :]
 
     def put_both(dst, row, v):
         for half in range(2):
@@ -370,15 +353,16 @@
         ]
         summed = jnp.dot(big[...], jnp.concatenate(taps, axis=1), preferred_element_type=F32)
         for r in range(8):
-            put_both(h_a, row + r, activate(summed[r * hid : (r + 1) * hid], ocean_row(row + r)))
-
-    src, dst = h_a, h_b
+            put_both(src, row + r, activate(summed[r * hid : (r + 1) * hid], ocean_row(row + r)))
+        yield
     for k in range(n_mid):
         cached = loader(src)
         for row in range(10 + k, 22 - k):
             taps = hidden_taps(cached, row, ALONG_Y)
             summed = jnp.dot(hidden[k], taps, preferred_element_type=F32)
             put_both(dst, row, activate(summed, ocean_row(row)))
+            if row % 2:
+                yield
         src, dst = dst, src
     slot = 2 * HALO
     cached = loader(src)
@@ -388,6 +372,45 @@
         for c in range(3):
             edge[c * slot + row - 13 : c * slot + row - 12, :] = v[c : c + 1, :span_y]
             edge[c * slot + row - 5 : c * slot + row - 4, :] = v[c : c + 1, span_y:]
+        if row % 2:
+            yield
+
+
+def edge_lines_kernel(
+    fields, mask, got_in, got_out, own_low, own_top, lat_in, lat_out, stress_in, kept, big, hidden, final, halved, out,
+    ext, ext_strip, rows_a, rows_b, h_a, h_b, stress, edge,
+):
+    feeds, span_x, span_y = fields.shape
+    lat, last = lax.axis_index("gy"), lax.axis_size("gy") - 1
+    odd = lax.rem(lat, 2) == 1
+    lower = lax.axis_index("gx") < lax.axis_size("gx") // 2
+    partner = jnp.where(jnp.where(lat == last, lower, odd), 1, 0)
+    stress[...] = stress_in[...]
+    west, own, east = sides(fields, mask, got_in, got_out)
+    for c in range(feeds + 1):
+        ext[c, :HALO] = west[c]
+        ext[c, HALO : HALO + span_x] = own[c]
+        ext[c, HALO + span_x :] = east[c]
+    ext_strip[...] = jnp.zeros_like(ext_strip)
+    for c in range(feeds + 1):
+        inner = lat_in[c].astype(F32)
+        outer = lat_out[partner, c].astype(F32)
+        outer = jnp.where(lat == 0, jnp.zeros_like(outer), outer)
+        below = jnp.where(odd, inner, outer)
+        above = jnp.where(odd, outer, inner)
+        ext_strip[c, 6:14, :span_y] = below
+        ext_strip[c, 14:30, :span_y] = own_low[c]
+        ext_strip[c, 2:18, span_y:] = own_top[c]
+        ext_strip[c, 18:26, span_y:] = above
+
+    todo = [
+        strip_layers(ext_strip, span_y, big, hidden, final, h_a, h_b, edge),
+        side_layers(ext, kept, span_x, big, hidden, final, rows_a, rows_b, stress),
+    ]
+    while todo:
+        todo = [layers for layers in todo if next(layers, todo) is None]
+
+    slot = 2 * HALO
     turned = edge[...].T[HALO - 1 : HALO + span_x + 1]
 
     half_x = halved[0:1, :]
@@ -431,10 +454,12 @@
 
 
 def outermost(fields, mask, metric):
+    feeds, span_x, span_y = fields.shape
+    columns = jnp.concatenate([fields[:, :HALO], fields[:, span_x - HALO :]], axis=1)
     return pl.pallas_call(
         edge_kernel,
         out_shape=[
-            jax.ShapeDtypeStruct((fields.shape[0] + 1, 2 * HALO, fields.shape[2]), BF16),
+            jax.ShapeDtypeStruct((feeds + 1, 2 * HALO, span_y), BF16),
             jax.ShapeDtypeStruct(metric.shape, F32),
         ],
         in_specs=[VMEM] * 3,
@@ -442,7 +467,7 @@
         compiler_params=pltpu.CompilerParams(vmem_limit_bytes=4 * 1024 * 1024),
         cost_estimate=pl.CostEstimate(flops=10_000_000_000, bytes_accessed=1_000_000, transcendentals=0),
         name="outermost_columns",
-    )(fields, mask, metric)
+    )(columns, mask, metric)
 
 
 def inner_shapes(fields, w_first, w_mid):
@@ -478,53 +503,55 @@
     )(edges, got_in, fields, mask, w_first, w_mid, w_last, biases)
 
 
-def side_columns(fields, mask, got_in, got_out, w_first, w_mid, w_last, biases, done):
+def late(fields, mask, w_first, w_mid, w_last, biases, done, lat_out):
     outs, scratch = inner_shapes(fields, w_first, w_mid)
-    hid, span_y = w_first.shape[2], mask.shape[1]
     return pl.pallas_call(
-        side_kernel,
-        out_shape=outs[:1] + outs[2:],
-        in_specs=[VMEM] * 13,
-        out_specs=[VMEM] * 4,
-        scratch_shapes=scratch
-        + [pltpu.VMEM((2, 3, 10, hid, span_y), BF16)] * 2
-        + [pltpu.VMEM(outs[1].shape, BF16)],
+        late_kernel,
+        out_shape=outs,
+        in_specs=[VMEM] * 12,
+        out_specs=[VMEM] * 5,
+        scratch_shapes=scratch,
         compiler_params=pltpu.CompilerParams(vmem_limit_bytes=12 * 1024 * 1024),
         cost_estimate=pl.CostEstimate(flops=5_000_000_000, bytes_accessed=20_000_000, transcendentals=0),
-        name="inner_and_sides",
-    )(fields, mask, got_in, got_out, w_first, w_mid, w_last, biases, *done)
-
-
-def strips(own_low, own_top, got_in, got_out, stress, big, hidden, final, mask, halved):
-    span_x, span_y = mask.shape
+        name="inner_late",
+    )(fields, mask, w_first, w_mid, w_last, biases, *done, lat_out)
+
+
+def edge_lines(fields, mask, got_in, got_out, own_low, own_top, lat_in, lat_out, inner, halved):
+    feeds, span_x, span_y = fields.shape
+    stress, _, _, hidden, _ = inner
     hid = hidden.shape[1]
     return pl.pallas_call(
-        strip_kernel,
+        edge_lines_kernel,
         out_shape=jax.ShapeDtypeStruct((2, span_x, span_y), F32),
-        in_specs=[VMEM] * 10,
+        in_specs=[VMEM] * 14,
         out_specs=VMEM,
         scratch_shapes=[
-            pltpu.VMEM((own_low.shape[0], STRIP, 2 * span_y), F32),
+            pltpu.VMEM((feeds + 1, span_x + 2 * HALO, span_y), F32),
+            pltpu.VMEM((feeds + 1, STRIP, 2 * span_y), F32),
+            pltpu.VMEM((2, 3, 10, hid, span_y), BF16),
+            pltpu.VMEM((2, 3, 10, hid, span_y), BF16),
             pltpu.VMEM((3, STRIP, hid, 2 * span_y), BF16),
             pltpu.VMEM((3, STRIP, hid, 2 * span_y), BF16),
+            pltpu.VMEM(stress.shape, F32),
             pltpu.VMEM((span_y, span_y), F32),
         ],
-        compiler_params=pltpu.CompilerParams(vmem_limit_bytes=8 * 1024 * 1024),
-        name="edge_rows",
-    )(own_low, own_top, got_in, got_out, stress, big, hidden, final, mask, halved)
-
-
-def latitude_pairs(count_x, count_y, across):
+        compiler_params=pltpu.CompilerParams(vmem_limit_bytes=12 * 1024 * 1024),
+        name="edge_lines",
+    )(fields, mask, got_in, got_out, own_low, own_top, lat_in, lat_out, *inner, halved)
+
+
+def latitude_swaps(count_x, count_y):
     at = lambda g, y: g * count_y + y
-    pairs = []
-    for g in range(count_x):
-        for y in range(count_y):
-            up = (y % 2 == 0) != across
-            if up and y == count_y - 1:
-                pairs.append((at(g, y), at(count_x - 1 - g, y)))
-            elif up or y > 0:
-                pairs.append((at(g, y), at(g, y + 1 if up else y - 1)))
-    return pairs
+    up = [(at(g, y), at(g, y + 1)) for g in range(count_x) for y in range(0, count_y, 2)]
+    return up + [(target, source) for source, target in up]
+
+
+def latitude_groups(count_x, count_y):
+    at = lambda g, y: g * count_y + y
+    pairs = [[at(g, y), at(g, y + 1)] for g in range(count_x) for y in range(1, count_y - 1, 2)]
+    pairs += [[at(g, count_y - 1), at(count_x - 1 - g, count_y - 1)] for g in range(count_x // 2)]
+    return pairs + [[at(g, 0), at((g + 1) % count_x, 0)] for g in range(1, count_x, 2)]
 
 
 def on_device(fields, ocean_mask, metric, w_first, w_mid, w_last, biases):
@@ -532,16 +559,15 @@
     inside = [[i, i + 1] for i in range(0, count_x, 2)]
     across = [[i, (i + 1) % count_x] for i in range(1, count_x, 2)]
     weights = (jnp.swapaxes(w_first, 1, 2), w_mid, w_last, biases)
-    ocean_mask = ocean_mask.astype(BF16)
     edges, halved = outermost(fields, ocean_mask, metric)
     got_in = lax.all_gather(edges, "gx", axis_index_groups=inside)
     edges, *done = early(edges, got_in, fields, ocean_mask, *weights)
     got_out = lax.all_gather(edges, "gx", axis_index_groups=across)
     pay_in, pay_out, own_low, own_top = pack(fields, ocean_mask, got_in, got_out)
-    lat_in = lax.ppermute(pay_in, ("gx", "gy"), latitude_pairs(count_x, count_y, False))
-    lat_out = lax.ppermute(pay_out, ("gx", "gy"), latitude_pairs(count_x, count_y, True))
-    stress, big, hidden, final = side_columns(fields, ocean_mask, got_in, got_out, *weights, done)
-    return strips(own_low, own_top, lat_in, lat_out, stress, big, hidden, final, ocean_mask, halved)
+    lat_in = lax.ppermute(pay_in, ("gx", "gy"), latitude_swaps(count_x, count_y))
+    lat_out = lax.all_gather(pay_out, ("gx", "gy"), axis_index_groups=latitude_groups(count_x, count_y))
+    inner = late(fields, ocean_mask, *weights, done, lat_out)
+    return edge_lines(fields, ocean_mask, got_in, got_out, own_low, own_top, lat_in, lat_out, inner, halved)
 
 
 def solution(mesh):

time: 35.5 us -> 34.6 us (0.975)
  blocking collectives: 14.8 us -> 21.9 us
  starting transfers between devices: 9.93 us -> 3.26 us
  Pallas kernels: 8.79 us -> 7.67 us
  other arithmetic: 0.78 us -> 0.01 us
  local copies, waits for them, and re-layouts: 0.86 us -> 1.42 us
    all_gather x0 -> x1, blocking collectives: none -> 7.13 us  [on_device(): lax.all_gather(pay_out, ('gx', 'gy'), axis_index_groups=latitude_groups(c...]
    ppermute x2 -> x1, starting transfers between devices: 9.93 us -> 3.26 us  [on_device(): lax.ppermute(pay_in, ('gx', 'gy'), latitude_swaps(count_x, count_y))]
    pallas_call x3, Pallas kernels: 4.37 us -> 3.23 us  [the longest x1 3.18 us: edge_lines(): pl.pallas_call(edge_lines_kernel, out_shape=jax.ShapeDtypeStruct((2, span...]
    convert_element_type x1 -> x0, other arithmetic: 0.78 us -> none  [on_device(): ocean_mask = ocean_mask.astype(BF16)]
    slice x0 -> x1, local copies, waits for them, and re-layouts: none -> 0.72 us  [outermost(): fields[:, :HALO]]
  transfers between devices with their start and end apart: 2 -> 1, of which waited for: 0 -> 0; matrix products, arithmetic and copies ran while one was open for 0% -> 0% of each run, Pallas kernels for 5% -> 0%
where the time goes in v2:
time: 34.6 us; the launch traced here: 34.4 us
  blocking collectives  21.9 us (63%)
  Pallas kernels  7.67 us (22%)
  starting transfers between devices  3.26 us (9%)
  local copies, waits for them, and re-layouts  1.42 us (4%)
    all_gather x1, blocking collectives, on_device(): got_out = lax.all_gather(edges, 'gx', axis_index_groups=across)  12.8 us
    all_gather x1, blocking collectives, on_device(): lax.all_gather(pay_out, ('gx', 'gy'), axis_index_groups=latitude_groups(c...  7.13 us
    pallas_call x1, Pallas kernels, early(): pl.pallas_call(early_kernel, out_shape=[jax.ShapeDtypeStruct(edges.shape,...  4.01 us
    ppermute x1, starting transfers between devices, on_device(): lax.ppermute(pay_in, ('gx', 'gy'), latitude_swaps(count_x, count_y))  3.26 us
    pallas_call x1, Pallas kernels, edge_lines(): pl.pallas_call(edge_lines_kernel, out_shape=jax.ShapeDtypeStruct((2, span...  3.18 us
    all_gather x1, blocking collectives, on_device(): got_in = lax.all_gather(edges, 'gx', axis_index_groups=inside)  1.97 us
    slice x1, local copies, waits for them, and re-layouts, outermost(): fields[:, :HALO]  0.72 us
    unnamed x14, local copies, waits for them, and re-layouts  0.7 us
  transfers between devices with their start and end apart: 1, of which 0 were waited for; matrix products, arithmetic and copies ran while one was open for 0% of the time, Pallas kernels for 0%

profile of v2, /device:TPU:56, one launch (start us, length us, event | category | flops | bytes accessed | tf_op | source)
XLA Modules:
  0.0 34.4 jit_solution(10003086443201409136)
XLA Ops:
  0.0 0.0 copy-start.1
  0.0 0.7 %fusion = (bf16[4,8,128]{2,1,0:T(8,128)(2,1)S(1)}, bf16[4,8,128]{2,1,0:T(8,128)(2,1)S(1)}) fusion(bf16[4,64,128]{2,1,0:T(8,128)(2,1)} %fields.7), kind=kLoop, calls=%fused_computation.1 | loop fusion | bytes 32768 | tf_op jit(solution)/shard_map/slice | solution.py:458
  0.7 0.0 copy-start.6
  0.7 0.1 copy-done.1
  0.8 0.6 %copy-done.6 = f32[2,128]{1,0:T(2,128)S(1)} copy-done((f32[2,128]{1,0:T(2,128)S(1)}, f32[2,128]{1,0:T(2,128)}, u32[]{:S(2)}) %copy-start.6) | copy-done | bytes 1048
  1.4 0.0 copy-start.2
  1.4 0.0 copy-start.3
  1.4 0.0 copy-start.4
  1.4 0.0 copy-start.5
  1.4 0.0 copy-start
  1.4 2.0 %all-gather = bf16[10,16,128]{2,1,0:T(8,128)(2,1)S(1)} all-gather(bf16[5,16,128]{2,1,0:T(8,128)(2,1)S(1)} %get-tuple-element.22.edges), channel_id=2, replica_groups={{0,8},{16,24},{32,40},{48,56},{64,72},{80,88},{96,104},{112,120},{128,1..., dimensions={0}, use_global_device_ids=true | all-gather | bytes 61440 | tf_op jit(solution)/shard_map/all_gather | solution.py:563
  3.4 0.0 copy-done.2
  3.4 0.0 copy-done.3
  3.4 0.0 copy-done.4
  3.4 0.0 copy-done.5
  3.4 0.0 copy-done
  3.4 4.0 %inner_early.1 = (bf16[5,16,128]{2,1,0:T(8,128)(2,1)S(1)}, f32[3,80,128]{2,1,0:T(8,128)S(1)}, bf16[4,4,48,128]{3,2,1,0:T(8,128)(2,1)S(1)}, bf16[384,176]{1,0:T(8...) custom-call(bf16[5,16,128]{2,1,0:T(8,128)(2,1)S(1)} %get-tuple-element.22.edges, ...), custom_call_target="tpu_custom_call" | custom-call | tf_op jit(solution)/shard_map/inner_early/pallas_call | solution.py:495
  7.5 12.8 %all-gather.1 = bf16[10,16,128]{2,1,0:T(8,128)(2,1)S(1)} all-gather(bf16[5,16,128]{2,1,0:T(8,128)(2,1)S(1)} %get-tuple-element.23), channel_id=3, replica_groups={{8,16},{24,32},{40,48},{56,64},{72,80},{88,96},{104,112},{120,128},{136..., dimensions={0}, use_global_device_ids=true | all-gather | bytes 61440 | tf_op jit(solution)/shard_map/all_gather | solution.py:565
  20.3 0.4 %pack_rows.1 = (bf16[5,8,128]{2,1,0:T(8,128)(2,1)S(1)}, bf16[5,8,128]{2,1,0:T(8,128)(2,1)S(1)}, f32[5,16,128]{2,1,0:T(8,128)S(1)}, f32[5,16,128]{2,1,0:T(8,128)S(1)}) custom-call(bf16[4,64,128]{2,1,0:T(8,128)(2,1)S(1)} %copy-done, s32[64,128]{1,0:T(8,128)S(1)} %copy-done.1, bf16[2,5,16,128]{3,2,1,0:T(8,128)(2,1)S(1)} %bitcast.5, ...), custom_call_target="tpu_custom_call" | custom-call | tf_op jit(solution)/shard_map/pack_rows/pallas_call | solution.py:445
  20.7 3.3 %collective-permute-start = (bf16[5,8,128]{2,1,0:T(8,128)(2,1)S(1)}, bf16[5,8,128]{2,1,0:T(8,128)(2,1)S(1)}, u32[]{:S(2)}, u32[]{:S(2)}) collective-permute-start(bf16[5,8,128]{2,1,0:T(8,128)(2,1)S(1)} %get-tuple-element.26), channel_id=1, source_target_pairs={{0,1},{2,3},{4,5},{6,7},{8,9},{10,11},{12,13},{14,15},{16,17},{18,... | collective-permute-start | bytes 30728 | tf_op jit(solution)/shard_map/ppermute | solution.py:567
  24.0 7.1 %all-gather.2 = bf16[10,8,128]{2,1,0:T(8,128)(2,1)S(1)} all-gather(bf16[5,8,128]{2,1,0:T(8,128)(2,1)S(1)} %get-tuple-element.27), channel_id=4, replica_groups={{1,2},{3,4},{5,6},{9,10},{11,12},{13,14},{17,18},{19,20},{21,22},{25,26..., dimensions={0}, use_global_device_ids=true | all-gather | bytes 30720 | tf_op jit(solution)/shard_map/all_gather | solution.py:568
  31.2 0.0 collective-permute-done.lat_in
  31.2 3.2 %edge_lines.1 = f32[2,64,128]{2,1,0:T(8,128)} custom-call(bf16[4,64,128]{2,1,0:T(8,128)(2,1)S(1)} %copy-done, s32[64,128]{1,0:T(8,128)S(1)} %copy-done.1, bf16[2,5,16,128]{3,2,1,0:T(8,128)(2,1)S(1)} %bitcast.6, bf16[2,5,16,128]{3,2,1,0:T(8,128)(2,1)S(1)} %bitcast.8, f32[5,16,128]{2,1,0:T(8,128)S(1)} %get-tuple-element.24.own_low, ...), custom_call_target="tpu_custom_call" | custom-call | tf_op jit(solution)/shard_map/edge_lines/pallas_call | solution.py:524
  (3 shorter events, 0.1 us)
Async XLA Ops:
  0.0 0.8 %copy-start.1 = (s32[64,128]{1,0:T(8,128)S(1)}, s32[64,128]{1,0:T(8,128)}, u32[]{:S(2)}) copy-start(s32[64,128]{1,0:T(8,128)} %mask.9) | copy-start | bytes 98308
  0.7 0.7 %copy-start.6 = (f32[2,128]{1,0:T(2,128)S(1)}, f32[2,128]{1,0:T(2,128)}, u32[]{:S(2)}) copy-start(f32[2,128]{1,0:T(2,128)} %metric.1) | copy-start | bytes 3076
  1.4 2.0 %copy-start.2 = (bf16[3,5,48,48]{3,2,1,0:T(8,128)(2,1)S(1)}, bf16[3,5,48,48]{3,2,1,0:T(8,128)(2,1)}, u32[]{:S(2)}) copy-start(bf16[3,5,48,48]{3,2,1,0:T(8,128)(2,1)} %w_mid.3) | copy-start | bytes 207364
  1.4 2.0 %copy-start.3 = (bf16[5,48,4]{1,2,0:T(4,128)(2,1)S(1)}, bf16[5,48,4]{1,2,0:T(4,128)(2,1)}, u32[]{:S(2)}) copy-start(bf16[5,48,4]{1,2,0:T(4,128)(2,1)} %param.10) | copy-start | bytes 5764
  1.4 2.0 %copy-start.4 = (bf16[5,3,48]{2,1,0:T(4,128)(2,1)S(1)}, bf16[5,3,48]{2,1,0:T(4,128)(2,1)}, u32[]{:S(2)}) copy-start(bf16[5,3,48]{2,1,0:T(4,128)(2,1)} %w_last.3) | copy-start | bytes 4324
  1.4 2.0 %copy-start.5 = (f32[4,48]{1,0:T(4,128)S(1)}, f32[4,48]{1,0:T(4,128)}, u32[]{:S(2)}) copy-start(f32[4,48]{1,0:T(4,128)} %biases.3) | copy-start | bytes 2308
  1.4 2.0 %copy-start = (bf16[4,64,128]{2,1,0:T(8,128)(2,1)S(1)}, bf16[4,64,128]{2,1,0:T(8,128)(2,1)}, u32[]{:S(2)}) copy-start(bf16[4,64,128]{2,1,0:T(8,128)(2,1)} %fields.7) | copy-start | bytes 196612
  20.7 10.4 %collective-permute-start = (bf16[5,8,128]{2,1,0:T(8,128)(2,1)S(1)}, bf16[5,8,128]{2,1,0:T(8,128)(2,1)S(1)}, u32[]{:S(2)}, u32[]{:S(2)}) collective-permute-start(bf16[5,8,128]{2,1,0:T(8,128)(2,1)S(1)} %get-tuple-element.26), channel_id=1, source_target_pairs={{0,1},{2,3},{4,5},{6,7},{8,9},{10,11},{12,13},{14,15},{16,17},{18,... | collective-permute-start | bytes 30728 | tf_op jit(solution)/shard_map/ppermute | solution.py:567

commit v3 on v2

--- a/solution.py
+++ b/solution.py
@@ -325,7 +325,7 @@
                     v = masked_stress(part, ocean_row(row))
                     for c in range(3):
                         stress[c, HALO + row : HALO + row + 1, :] = v[c : c + 1]
-            yield
+        yield
         if k < n_mid + 2:
             fill(dst, k)
         src, dst = dst, src
@@ -361,8 +361,7 @@
             taps = hidden_taps(cached, row, ALONG_Y)
             summed = jnp.dot(hidden[k], taps, preferred_element_type=F32)
             put_both(dst, row, activate(summed, ocean_row(row)))
-            if row % 2:
-                yield
+        yield
         src, dst = dst, src
     slot = 2 * HALO
     cached = loader(src)
@@ -391,7 +390,6 @@
         ext[c, :HALO] = west[c]
         ext[c, HALO : HALO + span_x] = own[c]
         ext[c, HALO + span_x :] = east[c]
-    ext_strip[...] = jnp.zeros_like(ext_strip)
     for c in range(feeds + 1):
         inner = lat_in[c].astype(F32)
         outer = lat_out[partner, c].astype(F32)

time: 34.6 us -> 34.5 us (level)
  no operation moved by 1% of the time
where the time goes in v3:
time: 34.5 us; the launch traced here: 34.2 us
  blocking collectives  21.9 us (63%)
  Pallas kernels  7.56 us (22%)
  starting transfers between devices  3.26 us (9%)
  local copies, waits for them, and re-layouts  1.42 us (4%)
    all_gather x1, blocking collectives, on_device(): got_out = lax.all_gather(edges, 'gx', axis_index_groups=across)  12.8 us
    all_gather x1, blocking collectives, on_device(): lax.all_gather(pay_out, ('gx', 'gy'), axis_index_groups=latitude_groups(c...  7.13 us
    pallas_call x1, Pallas kernels, early(): pl.pallas_call(early_kernel, out_shape=[jax.ShapeDtypeStruct(edges.shape,...  4.01 us
    ppermute x1, starting transfers between devices, on_device(): lax.ppermute(pay_in, ('gx', 'gy'), latitude_swaps(count_x, count_y))  3.26 us
    pallas_call x1, Pallas kernels, edge_lines(): pl.pallas_call(edge_lines_kernel, out_shape=jax.ShapeDtypeStruct((2, span...  3.08 us
    all_gather x1, blocking collectives, on_device(): got_in = lax.all_gather(edges, 'gx', axis_index_groups=inside)  1.97 us
    slice x1, local copies, waits for them, and re-layouts, outermost(): fields[:, :HALO]  0.72 us
    unnamed x14, local copies, waits for them, and re-layouts  0.7 us
  transfers between devices with their start and end apart: 1, of which 0 were waited for; matrix products, arithmetic and copies ran while one was open for 0% of the time, Pallas kernels for 0%

profile of v3, /device:TPU:56, one launch (start us, length us, event | category | flops | bytes accessed | tf_op | source)
XLA Modules:
  0.0 34.2 jit_solution(11534755825672687405)
XLA Ops:
  0.0 0.0 copy-start.1
  0.0 0.7 %fusion = (bf16[4,8,128]{2,1,0:T(8,128)(2,1)S(1)}, bf16[4,8,128]{2,1,0:T(8,128)(2,1)S(1)}) fusion(bf16[4,64,128]{2,1,0:T(8,128)(2,1)} %fields.7), kind=kLoop, calls=%fused_computation.1 | loop fusion | bytes 32768 | tf_op jit(solution)/shard_map/slice | solution.py:456
  0.7 0.0 copy-start.6
  0.7 0.1 copy-done.1
  0.8 0.6 %copy-done.6 = f32[2,128]{1,0:T(2,128)S(1)} copy-done((f32[2,128]{1,0:T(2,128)S(1)}, f32[2,128]{1,0:T(2,128)}, u32[]{:S(2)}) %copy-start.6) | copy-done | bytes 1048
  1.4 0.0 copy-start.2
  1.4 0.0 copy-start.3
  1.4 0.0 copy-start.4
  1.4 0.0 copy-start.5
  1.4 0.0 copy-start
  1.4 2.0 %all-gather = bf16[10,16,128]{2,1,0:T(8,128)(2,1)S(1)} all-gather(bf16[5,16,128]{2,1,0:T(8,128)(2,1)S(1)} %get-tuple-element.22.edges), channel_id=2, replica_groups={{0,8},{16,24},{32,40},{48,56},{64,72},{80,88},{96,104},{112,120},{128,1..., dimensions={0}, use_global_device_ids=true | all-gather | bytes 61440 | tf_op jit(solution)/shard_map/all_gather | solution.py:561
  3.4 0.0 copy-done.2
  3.4 0.0 copy-done.3
  3.4 0.0 copy-done.4
  3.4 0.0 copy-done.5
  3.4 0.0 copy-done
  3.4 4.0 %inner_early.1 = (bf16[5,16,128]{2,1,0:T(8,128)(2,1)S(1)}, f32[3,80,128]{2,1,0:T(8,128)S(1)}, bf16[4,4,48,128]{3,2,1,0:T(8,128)(2,1)S(1)}, bf16[384,176]{1,0:T(8...) custom-call(bf16[5,16,128]{2,1,0:T(8,128)(2,1)S(1)} %get-tuple-element.22.edges, ...), custom_call_target="tpu_custom_call" | custom-call | tf_op jit(solution)/shard_map/inner_early/pallas_call | solution.py:493
  7.5 12.8 %all-gather.1 = bf16[10,16,128]{2,1,0:T(8,128)(2,1)S(1)} all-gather(bf16[5,16,128]{2,1,0:T(8,128)(2,1)S(1)} %get-tuple-element.23), channel_id=3, replica_groups={{8,16},{24,32},{40,48},{56,64},{72,80},{88,96},{104,112},{120,128},{136..., dimensions={0}, use_global_device_ids=true | all-gather | bytes 61440 | tf_op jit(solution)/shard_map/all_gather | solution.py:563
  20.3 0.4 %pack_rows.1 = (bf16[5,8,128]{2,1,0:T(8,128)(2,1)S(1)}, bf16[5,8,128]{2,1,0:T(8,128)(2,1)S(1)}, f32[5,16,128]{2,1,0:T(8,128)S(1)}, f32[5,16,128]{2,1,0:T(8,128)S(1)}) custom-call(bf16[4,64,128]{2,1,0:T(8,128)(2,1)S(1)} %copy-done, s32[64,128]{1,0:T(8,128)S(1)} %copy-done.1, bf16[2,5,16,128]{3,2,1,0:T(8,128)(2,1)S(1)} %bitcast.5, ...), custom_call_target="tpu_custom_call" | custom-call | tf_op jit(solution)/shard_map/pack_rows/pallas_call | solution.py:443
  20.7 3.3 %collective-permute-start = (bf16[5,8,128]{2,1,0:T(8,128)(2,1)S(1)}, bf16[5,8,128]{2,1,0:T(8,128)(2,1)S(1)}, u32[]{:S(2)}, u32[]{:S(2)}) collective-permute-start(bf16[5,8,128]{2,1,0:T(8,128)(2,1)S(1)} %get-tuple-element.26), channel_id=1, source_target_pairs={{0,1},{2,3},{4,5},{6,7},{8,9},{10,11},{12,13},{14,15},{16,17},{18,... | collective-permute-start | bytes 30728 | tf_op jit(solution)/shard_map/ppermute | solution.py:565
  24.0 7.1 %all-gather.2 = bf16[10,8,128]{2,1,0:T(8,128)(2,1)S(1)} all-gather(bf16[5,8,128]{2,1,0:T(8,128)(2,1)S(1)} %get-tuple-element.27), channel_id=4, replica_groups={{1,2},{3,4},{5,6},{9,10},{11,12},{13,14},{17,18},{19,20},{21,22},{25,26..., dimensions={0}, use_global_device_ids=true | all-gather | bytes 30720 | tf_op jit(solution)/shard_map/all_gather | solution.py:566
  31.2 0.0 collective-permute-done.lat_in
  31.2 3.1 %edge_lines.1 = f32[2,64,128]{2,1,0:T(8,128)} custom-call(bf16[4,64,128]{2,1,0:T(8,128)(2,1)S(1)} %copy-done, s32[64,128]{1,0:T(8,128)S(1)} %copy-done.1, bf16[2,5,16,128]{3,2,1,0:T(8,128)(2,1)S(1)} %bitcast.6, bf16[2,5,16,128]{3,2,1,0:T(8,128)(2,1)S(1)} %bitcast.8, f32[5,16,128]{2,1,0:T(8,128)S(1)} %get-tuple-element.24.own_low, ...), custom_call_target="tpu_custom_call" | custom-call | tf_op jit(solution)/shard_map/edge_lines/pallas_call | solution.py:522
  (3 shorter events, 0.1 us)
Async XLA Ops:
  0.0 0.8 %copy-start.1 = (s32[64,128]{1,0:T(8,128)S(1)}, s32[64,128]{1,0:T(8,128)}, u32[]{:S(2)}) copy-start(s32[64,128]{1,0:T(8,128)} %mask.9) | copy-start | bytes 98308
  0.7 0.7 %copy-start.6 = (f32[2,128]{1,0:T(2,128)S(1)}, f32[2,128]{1,0:T(2,128)}, u32[]{:S(2)}) copy-start(f32[2,128]{1,0:T(2,128)} %metric.1) | copy-start | bytes 3076
  1.4 2.0 %copy-start.2 = (bf16[3,5,48,48]{3,2,1,0:T(8,128)(2,1)S(1)}, bf16[3,5,48,48]{3,2,1,0:T(8,128)(2,1)}, u32[]{:S(2)}) copy-start(bf16[3,5,48,48]{3,2,1,0:T(8,128)(2,1)} %w_mid.3) | copy-start | bytes 207364
  1.4 2.0 %copy-start.3 = (bf16[5,48,4]{1,2,0:T(4,128)(2,1)S(1)}, bf16[5,48,4]{1,2,0:T(4,128)(2,1)}, u32[]{:S(2)}) copy-start(bf16[5,48,4]{1,2,0:T(4,128)(2,1)} %param.10) | copy-start | bytes 5764
  1.4 2.0 %copy-start.4 = (bf16[5,3,48]{2,1,0:T(4,128)(2,1)S(1)}, bf16[5,3,48]{2,1,0:T(4,128)(2,1)}, u32[]{:S(2)}) copy-start(bf16[5,3,48]{2,1,0:T(4,128)(2,1)} %w_last.3) | copy-start | bytes 4324
  1.4 2.0 %copy-start.5 = (f32[4,48]{1,0:T(4,128)S(1)}, f32[4,48]{1,0:T(4,128)}, u32[]{:S(2)}) copy-start(f32[4,48]{1,0:T(4,128)} %biases.3) | copy-start | bytes 2308
  1.4 2.0 %copy-start = (bf16[4,64,128]{2,1,0:T(8,128)(2,1)S(1)}, bf16[4,64,128]{2,1,0:T(8,128)(2,1)}, u32[]{:S(2)}) copy-start(bf16[4,64,128]{2,1,0:T(8,128)(2,1)} %fields.7) | copy-start | bytes 196612
  20.7 10.4 %collective-permute-start = (bf16[5,8,128]{2,1,0:T(8,128)(2,1)S(1)}, bf16[5,8,128]{2,1,0:T(8,128)(2,1)S(1)}, u32[]{:S(2)}, u32[]{:S(2)}) collective-permute-start(bf16[5,8,128]{2,1,0:T(8,128)(2,1)S(1)} %get-tuple-element.26), channel_id=1, source_target_pairs={{0,1},{2,3},{4,5},{6,7},{8,9},{10,11},{12,13},{14,15},{16,17},{18,... | collective-permute-start | bytes 30728 | tf_op jit(solution)/shard_map/ppermute | solution.py:565

commit v4 on v3

--- a/solution.py
+++ b/solution.py
@@ -35,13 +35,14 @@
     return west, own, east
 
 
-def edge_kernel(columns, mask, metric, edges, halved):
-    feeds = columns.shape[0]
-    span_x = mask.shape[0]
-    edges[:feeds] = columns[...]
+def edge_kernel(fields, mask, metric, biases, edges, halved, own_biases):
+    feeds, span_x, _ = fields.shape
     for part, start in enumerate((0, span_x - HALO)):
-        edges[feeds, part * HALO : (part + 1) * HALO] = mask[start : start + HALO].astype(F32).astype(BF16)
+        rows = slice(part * HALO, (part + 1) * HALO)
+        edges[:feeds, rows] = fields[:, start : start + HALO].astype(BF16)
+        edges[feeds, rows] = mask[start : start + HALO].astype(F32).astype(BF16)
     halved[...] = metric[...] * 0.5
+    own_biases[...] = biases[...]
 
 
 def pack_kernel(fields, mask, got_in, got_out, pay_in, pay_out, own_low, own_top):
@@ -451,21 +452,37 @@
     )(fields, mask, got_in, got_out)
 
 
-def outermost(fields, mask, metric):
+def outermost(fields, mask, metric, biases):
     feeds, span_x, span_y = fields.shape
-    columns = jnp.concatenate([fields[:, :HALO], fields[:, span_x - HALO :]], axis=1)
     return pl.pallas_call(
         edge_kernel,
         out_shape=[
             jax.ShapeDtypeStruct((feeds + 1, 2 * HALO, span_y), BF16),
             jax.ShapeDtypeStruct(metric.shape, F32),
+            jax.ShapeDtypeStruct(biases.shape, F32),
         ],
-        in_specs=[VMEM] * 3,
-        out_specs=[VMEM] * 2,
+        in_specs=[VMEM] * 4,
+        out_specs=[VMEM] * 3,
         compiler_params=pltpu.CompilerParams(vmem_limit_bytes=4 * 1024 * 1024),
         cost_estimate=pl.CostEstimate(flops=10_000_000_000, bytes_accessed=1_000_000, transcendentals=0),
         name="outermost_columns",
-    )(columns, mask, metric)
+    )(fields, mask, metric, biases)
+
+
+def hold_kernel(edges, edges_out):
+    edges_out[...] = edges[...]
+
+
+def hold(edges):
+    return pl.pallas_call(
+        hold_kernel,
+        out_shape=jax.ShapeDtypeStruct(edges.shape, edges.dtype),
+        in_specs=[VMEM],
+        out_specs=VMEM,
+        compiler_params=pltpu.CompilerParams(vmem_limit_bytes=4 * 1024 * 1024),
+        cost_estimate=pl.CostEstimate(flops=10_000_000_000, bytes_accessed=1_000_000, transcendentals=0),
+        name="hold",
+    )(edges)
 
 
 def inner_shapes(fields, w_first, w_mid):
@@ -556,8 +573,10 @@
     count_x, count_y = lax.axis_size("gx"), lax.axis_size("gy")
     inside = [[i, i + 1] for i in range(0, count_x, 2)]
     across = [[i, (i + 1) % count_x] for i in range(1, count_x, 2)]
+    fields = fields.astype(F32)
+    edges, halved, biases = outermost(fields, ocean_mask, metric, biases)
     weights = (jnp.swapaxes(w_first, 1, 2), w_mid, w_last, biases)
-    edges, halved = outermost(fields, ocean_mask, metric)
+    edges = hold(hold(edges))
     got_in = lax.all_gather(edges, "gx", axis_index_groups=inside)
     edges, *done = early(edges, got_in, fields, ocean_mask, *weights)
     got_out = lax.all_gather(edges, "gx", axis_index_groups=across)

time: 34.5 us -> 34.7 us (level)
  other arithmetic: 0.01 us -> 0.89 us
  local copies, waits for them, and re-layouts: 1.42 us -> 0.71 us
    convert_element_type x0 -> x1, other arithmetic: none -> 0.89 us  [on_device(): fields = fields.astype(F32)]
    slice x1 -> x0, local copies, waits for them, and re-layouts: 0.72 us -> none  [outermost(): fields[:, :HALO]]
    unnamed x14 -> x12, local copies, waits for them, and re-layouts: 0.7 us -> 0.71 us
where the time goes in v4:
time: 34.7 us; the launch traced here: 34.4 us
  blocking collectives  21.9 us (63%)
  Pallas kernels  7.61 us (22%)
  starting transfers between devices  3.26 us (9%)
  other arithmetic  0.89 us (3%)
  local copies, waits for them, and re-layouts  0.71 us (2%)
    all_gather x1, blocking collectives, on_device(): got_out = lax.all_gather(edges, 'gx', axis_index_groups=across)  12.8 us
    all_gather x1, blocking collectives, on_device(): lax.all_gather(pay_out, ('gx', 'gy'), axis_index_groups=latitude_groups(c...  7.13 us
    pallas_call x1, Pallas kernels, early(): pl.pallas_call(early_kernel, out_shape=[jax.ShapeDtypeStruct(edges.shape,...  4.02 us
    ppermute x1, starting transfers between devices, on_device(): lax.ppermute(pay_in, ('gx', 'gy'), latitude_swaps(count_x, count_y))  3.26 us
    pallas_call x1, Pallas kernels, edge_lines(): pl.pallas_call(edge_lines_kernel, out_shape=jax.ShapeDtypeStruct((2, span...  3.11 us
    all_gather x1, blocking collectives, on_device(): got_in = lax.all_gather(edges, 'gx', axis_index_groups=inside)  1.97 us
    convert_element_type x1, other arithmetic, on_device(): fields = fields.astype(F32)  0.89 us
    unnamed x12, local copies, waits for them, and re-layouts  0.71 us
  transfers between devices with their start and end apart: 1, of which 0 were waited for; matrix products, arithmetic and copies ran while one was open for 0% of the time, Pallas kernels for 0%

profile of v4, /device:TPU:56, one launch (start us, length us, event | category | flops | bytes accessed | tf_op | source)
XLA Modules:
  0.0 34.4 jit_solution(10787484741052642337)
XLA Ops:
  0.0 0.0 copy-start
  0.0 0.0 copy-start.4
  0.0 0.0 copy-start.5
  0.0 0.9 %convert_element_type.3.fields = f32[4,64,128]{2,1,0:T(8,128)S(1)} convert(bf16[4,64,128]{2,1,0:T(8,128)(2,1)} %param.7) | non-fusion elementwise | flops 32768 | bytes 196608 | tf_op jit(solution)/shard_map/convert_element_type | solution.py:576
  0.9 0.0 copy-done
  0.9 0.0 copy-done.4
  0.9 0.0 copy-done.5
  1.0 0.0 copy-start.1
  1.0 0.0 copy-start.3
  1.0 2.0 %all-gather = bf16[10,16,128]{2,1,0:T(8,128)(2,1)S(1)} all-gather(bf16[5,16,128]{2,1,0:T(8,128)(2,1)S(1)} %hold.3.edges), channel_id=2, replica_groups={{0,8},{16,24},{32,40},{48,56},{64,72},{80,88},{96,104},{112,120},{128,1..., dimensions={0}, use_global_device_ids=true | all-gather | bytes 61440 | tf_op jit(solution)/shard_map/all_gather | solution.py:580
  3.0 0.0 copy-start.2
  3.0 0.0 copy-done.1
  3.0 0.0 copy-done.3
  3.0 0.7 %copy-done.2 = bf16[5,48,4]{1,2,0:T(4,128)(2,1)S(1)} copy-done((bf16[5,48,4]{1,2,0:T(4,128)(2,1)S(1)}, bf16[5,48,4]{1,2,0:T(4,128)(2,1)}, u32[]{:S(2)}) %copy-start.2) | copy-done | bytes 1944
  3.7 4.0 %inner_early.1 = (bf16[5,16,128]{2,1,0:T(8,128)(2,1)S(1)}, f32[3,80,128]{2,1,0:T(8,128)S(1)}, bf16[4,4,48,128]{3,2,1,0:T(8,128)(2,1)S(1)}, bf16[384,176]{1,0:T(8...) custom-call(bf16[5,16,128]{2,1,0:T(8,128)(2,1)S(1)} %hold.3.edges, ...), custom_call_target="tpu_custom_call" | custom-call | tf_op jit(solution)/shard_map/inner_early/pallas_call | solution.py:510
  7.7 12.8 %all-gather.1 = bf16[10,16,128]{2,1,0:T(8,128)(2,1)S(1)} all-gather(bf16[5,16,128]{2,1,0:T(8,128)(2,1)S(1)} %get-tuple-element.25), channel_id=3, replica_groups={{8,16},{24,32},{40,48},{56,64},{72,80},{88,96},{104,112},{120,128},{136..., dimensions={0}, use_global_device_ids=true | all-gather | bytes 61440 | tf_op jit(solution)/shard_map/all_gather | solution.py:582
  20.4 0.4 %pack_rows.1 = (bf16[5,8,128]{2,1,0:T(8,128)(2,1)S(1)}, bf16[5,8,128]{2,1,0:T(8,128)(2,1)S(1)}, f32[5,16,128]{2,1,0:T(8,128)S(1)}, f32[5,16,128]{2,1,0:T(8,128)S(1)}) custom-call(f32[4,64,128]{2,1,0:T(8,128)S(1)} %convert_element_type.3.fields, s32[64,128]{1,0:T(8,128)S(1)} %copy-done, bf16[2,5,16,128]{3,2,1,0:T(8,128)(2,1)S(1)} %bitcast.5, ...), custom_call_target="tpu_custom_call" | custom-call | tf_op jit(solution)/shard_map/pack_rows/pallas_call | solution.py:444
  20.9 3.3 %collective-permute-start = (bf16[5,8,128]{2,1,0:T(8,128)(2,1)S(1)}, bf16[5,8,128]{2,1,0:T(8,128)(2,1)S(1)}, u32[]{:S(2)}, u32[]{:S(2)}) collective-permute-start(bf16[5,8,128]{2,1,0:T(8,128)(2,1)S(1)} %get-tuple-element.28), channel_id=1, source_target_pairs={{0,1},{2,3},{4,5},{6,7},{8,9},{10,11},{12,13},{14,15},{16,17},{18,... | collective-permute-start | bytes 30728 | tf_op jit(solution)/shard_map/ppermute | solution.py:584
  24.1 7.1 %all-gather.2 = bf16[10,8,128]{2,1,0:T(8,128)(2,1)S(1)} all-gather(bf16[5,8,128]{2,1,0:T(8,128)(2,1)S(1)} %get-tuple-element.29), channel_id=4, replica_groups={{1,2},{3,4},{5,6},{9,10},{11,12},{13,14},{17,18},{19,20},{21,22},{25,26..., dimensions={0}, use_global_device_ids=true | all-gather | bytes 30720 | tf_op jit(solution)/shard_map/all_gather | solution.py:585
  31.3 0.0 collective-permute-done.lat_in
  31.3 3.1 %edge_lines.1 = f32[2,64,128]{2,1,0:T(8,128)} custom-call(f32[4,64,128]{2,1,0:T(8,128)S(1)} %convert_element_type.3.fields, s32[64,128]{1,0:T(8,128)S(1)} %copy-done, bf16[2,5,16,128]{3,2,1,0:T(8,128)(2,1)S(1)} %bitcast.6, bf16[2,5,16,128]{3,2,1,0:T(8,128)(2,1)S(1)} %bitcast.8, f32[5,16,128]{2,1,0:T(8,128)S(1)} %get-tuple-element.26.own_low, ...), custom_call_target="tpu_custom_call" | custom-call | tf_op jit(solution)/shard_map/edge_lines/pallas_call | solution.py:539
  (4 shorter events, 0.1 us)
Async XLA Ops:
  0.0 0.9 %copy-start = (s32[64,128]{1,0:T(8,128)S(1)}, s32[64,128]{1,0:T(8,128)}, u32[]{:S(2)}) copy-start(s32[64,128]{1,0:T(8,128)} %mask.9) | copy-start | bytes 98308
  0.0 0.9 %copy-start.4 = (f32[4,48]{1,0:T(4,128)S(1)}, f32[4,48]{1,0:T(4,128)}, u32[]{:S(2)}) copy-start(f32[4,48]{1,0:T(4,128)} %biases.1) | copy-start | bytes 2308
  0.0 0.9 %copy-start.5 = (f32[2,128]{1,0:T(2,128)S(1)}, f32[2,128]{1,0:T(2,128)}, u32[]{:S(2)}) copy-start(f32[2,128]{1,0:T(2,128)} %metric.1) | copy-start | bytes 3076
  1.0 2.0 %copy-start.1 = (bf16[3,5,48,48]{3,2,1,0:T(8,128)(2,1)S(1)}, bf16[3,5,48,48]{3,2,1,0:T(8,128)(2,1)}, u32[]{:S(2)}) copy-start(bf16[3,5,48,48]{3,2,1,0:T(8,128)(2,1)} %w_mid.3) | copy-start | bytes 207364
  1.0 2.0 %copy-start.3 = (bf16[5,3,48]{2,1,0:T(4,128)(2,1)S(1)}, bf16[5,3,48]{2,1,0:T(4,128)(2,1)}, u32[]{:S(2)}) copy-start(bf16[5,3,48]{2,1,0:T(4,128)(2,1)} %w_last.3) | copy-start | bytes 4324
  3.0 0.7 %copy-start.2 = (bf16[5,48,4]{1,2,0:T(4,128)(2,1)S(1)}, bf16[5,48,4]{1,2,0:T(4,128)(2,1)}, u32[]{:S(2)}) copy-start(bf16[5,48,4]{1,2,0:T(4,128)(2,1)} %param.10) | copy-start | bytes 5764
  20.9 10.4 %collective-permute-start = (bf16[5,8,128]{2,1,0:T(8,128)(2,1)S(1)}, bf16[5,8,128]{2,1,0:T(8,128)(2,1)S(1)}, u32[]{:S(2)}, u32[]{:S(2)}) collective-permute-start(bf16[5,8,128]{2,1,0:T(8,128)(2,1)S(1)} %get-tuple-element.28), channel_id=1, source_target_pairs={{0,1},{2,3},{4,5},{6,7},{8,9},{10,11},{12,13},{14,15},{16,17},{18,... | collective-permute-start | bytes 30728 | tf_op jit(solution)/shard_map/ppermute | solution.py:584

commit v5 on v3

--- a/solution.py
+++ b/solution.py
@@ -25,22 +25,25 @@
     odd = lax.rem(lax.axis_index("gx"), 2)
     west, own, east = [], [], []
     for c in range(chans):
-        near = got_in[1 - odd, c]
-        far = got_out[odd, c]
-        near_low, near_high = near[:HALO].astype(F32), near[HALO:].astype(F32)
-        far_low, far_high = far[:HALO].astype(F32), far[HALO:].astype(F32)
-        west.append(jnp.where(odd == 1, near_high, far_high))
-        east.append(jnp.where(odd == 1, far_low, near_low))
+        near = got_in[1 - odd, c].astype(F32)
+        far = got_out[odd, c].astype(F32)
+        west.append(jnp.where(odd == 1, near, far))
+        east.append(jnp.where(odd == 1, far, near))
         own.append(fields[c].astype(F32) if c < chans - 1 else mask[...].astype(F32))
     return west, own, east
 
 
-def edge_kernel(columns, mask, metric, edges, halved):
+def edge_kernel(columns, mask, metric, edges_in, edges_out, halved):
     feeds = columns.shape[0]
     span_x = mask.shape[0]
-    edges[:feeds] = columns[...]
-    for part, start in enumerate((0, span_x - HALO)):
-        edges[feeds, part * HALO : (part + 1) * HALO] = mask[start : start + HALO].astype(F32).astype(BF16)
+    odd = lax.rem(lax.axis_index("gx"), 2) == 1
+    for c in range(feeds + 1):
+        if c < feeds:
+            low, high = columns[c, :HALO].astype(F32), columns[c, HALO:].astype(F32)
+        else:
+            low, high = mask[:HALO].astype(F32), mask[span_x - HALO :].astype(F32)
+        edges_in[c] = jnp.where(odd, low, high).astype(BF16)
+        edges_out[c] = jnp.where(odd, high, low).astype(BF16)
     halved[...] = metric[...] * 0.5
 
 
@@ -457,11 +460,12 @@
     return pl.pallas_call(
         edge_kernel,
         out_shape=[
-            jax.ShapeDtypeStruct((feeds + 1, 2 * HALO, span_y), BF16),
+            jax.ShapeDtypeStruct((feeds + 1, HALO, span_y), BF16),
+            jax.ShapeDtypeStruct((feeds + 1, HALO, span_y), BF16),
             jax.ShapeDtypeStruct(metric.shape, F32),
         ],
         in_specs=[VMEM] * 3,
-        out_specs=[VMEM] * 2,
+        out_specs=[VMEM] * 3,
         compiler_params=pltpu.CompilerParams(vmem_limit_bytes=4 * 1024 * 1024),
         cost_estimate=pl.CostEstimate(flops=10_000_000_000, bytes_accessed=1_000_000, transcendentals=0),
         name="outermost_columns",
@@ -557,8 +561,8 @@
     inside = [[i, i + 1] for i in range(0, count_x, 2)]
     across = [[i, (i + 1) % count_x] for i in range(1, count_x, 2)]
     weights = (jnp.swapaxes(w_first, 1, 2), w_mid, w_last, biases)
-    edges, halved = outermost(fields, ocean_mask, metric)
-    got_in = lax.all_gather(edges, "gx", axis_index_groups=inside)
+    edges_in, edges, halved = outermost(fields, ocean_mask, metric)
+    got_in = lax.all_gather(edges_in, "gx", axis_index_groups=inside)
     edges, *done = early(edges, got_in, fields, ocean_mask, *weights)
     got_out = lax.all_gather(edges, "gx", axis_index_groups=across)
     pay_in, pay_out, own_low, own_top = pack(fields, ocean_mask, got_in, got_out)

time: 34.5 us -> 35.1 us (1.017)
  local copies, waits for them, and re-layouts: 1.42 us -> 2.08 us
    unnamed x14, local copies, waits for them, and re-layouts: 0.7 us -> 1.35 us
where the time goes in v5:
time: 35.1 us; the launch traced here: 34.8 us
  blocking collectives  21.8 us (62%)
  Pallas kernels  7.56 us (22%)
  starting transfers between devices  3.26 us (9%)
  local copies, waits for them, and re-layouts  2.08 us (6%)
    all_gather x1, blocking collectives, on_device(): got_out = lax.all_gather(edges, 'gx', axis_index_groups=across)  12.7 us
    all_gather x1, blocking collectives, on_device(): lax.all_gather(pay_out, ('gx', 'gy'), axis_index_groups=latitude_groups(c...  7.13 us
    pallas_call x1, Pallas kernels, early(): pl.pallas_call(early_kernel, out_shape=[jax.ShapeDtypeStruct(edges.shape,...  3.98 us
    ppermute x1, starting transfers between devices, on_device(): lax.ppermute(pay_in, ('gx', 'gy'), latitude_swaps(count_x, count_y))  3.26 us
    pallas_call x1, Pallas kernels, edge_lines(): pl.pallas_call(edge_lines_kernel, out_shape=jax.ShapeDtypeStruct((2, span...  3.09 us
    all_gather x1, blocking collectives, on_device(): got_in = lax.all_gather(edges_in, 'gx', axis_index_groups=inside)  1.95 us
    unnamed x14, local copies, waits for them, and re-layouts  1.35 us
    slice x1, local copies, waits for them, and re-layouts, outermost(): fields[:, :HALO]  0.72 us
  transfers between devices with their start and end apart: 1, of which 0 were waited for; matrix products, arithmetic and copies ran while one was open for 0% of the time, Pallas kernels for 0%

profile of v5, /device:TPU:56, one launch (start us, length us, event | category | flops | bytes accessed | tf_op | source)
XLA Modules:
  0.0 34.8 jit_solution(17260603203070774207)
XLA Ops:
  0.0 0.0 copy-start.1
  0.0 0.7 %fusion = (bf16[4,8,128]{2,1,0:T(8,128)(2,1)S(1)}, bf16[4,8,128]{2,1,0:T(8,128)(2,1)S(1)}) fusion(bf16[4,64,128]{2,1,0:T(8,128)(2,1)} %fields.7), kind=kLoop, calls=%fused_computation.1 | loop fusion | bytes 32768 | tf_op jit(solution)/shard_map/slice | solution.py:459
  0.7 0.0 copy-start.6
  0.7 0.1 copy-done.1
  0.8 0.6 %copy-done.6 = f32[2,128]{1,0:T(2,128)S(1)} copy-done((f32[2,128]{1,0:T(2,128)S(1)}, f32[2,128]{1,0:T(2,128)}, u32[]{:S(2)}) %copy-start.6) | copy-done | bytes 1048
  1.4 0.0 copy-start
  1.4 0.0 copy-start.2
  1.4 0.0 copy-start.5
  1.4 0.0 copy-start.4
  1.5 2.0 %all-gather = bf16[10,8,128]{2,1,0:T(8,128)(2,1)S(1)} all-gather(bf16[5,8,128]{2,1,0:T(8,128)(2,1)S(1)} %get-tuple-element.23), channel_id=2, replica_groups={{0,8},{16,24},{32,40},{48,56},{64,72},{80,88},{96,104},{112,120},{128,1..., dimensions={0}, use_global_device_ids=true | all-gather | bytes 30720 | tf_op jit(solution)/shard_map/all_gather | solution.py:565
  3.4 0.0 copy-start.3
  3.4 0.0 copy-done
  3.4 0.0 copy-done.2
  3.4 0.0 copy-done.5
  3.4 0.0 copy-done.4
  3.4 0.7 %copy-done.3 = bf16[5,48,4]{1,2,0:T(4,128)(2,1)S(1)} copy-done((bf16[5,48,4]{1,2,0:T(4,128)(2,1)S(1)}, bf16[5,48,4]{1,2,0:T(4,128)(2,1)}, u32[]{:S(2)}) %copy-start.3) | copy-done | bytes 1944
  4.1 4.0 %inner_early.1 = (bf16[5,8,128]{2,1,0:T(8,128)(2,1)S(1)}, f32[3,80,128]{2,1,0:T(8,128)S(1)}, bf16[4,4,48,128]{3,2,1,0:T(8,128)(2,1)S(1)}, bf16[384,176]{1,0:T(8,...) custom-call(bf16[5,8,128]{2,1,0:T(8,128)(2,1)S(1)} %get-tuple-element.24.edges, ...), custom_call_target="tpu_custom_call" | custom-call | tf_op jit(solution)/shard_map/inner_early/pallas_call | solution.py:497
  8.1 12.7 %all-gather.1 = bf16[10,8,128]{2,1,0:T(8,128)(2,1)S(1)} all-gather(bf16[5,8,128]{2,1,0:T(8,128)(2,1)S(1)} %get-tuple-element.25), channel_id=3, replica_groups={{8,16},{24,32},{40,48},{56,64},{72,80},{88,96},{104,112},{120,128},{136..., dimensions={0}, use_global_device_ids=true | all-gather | bytes 30720 | tf_op jit(solution)/shard_map/all_gather | solution.py:567
  20.8 0.4 %pack_rows.1 = (bf16[5,8,128]{2,1,0:T(8,128)(2,1)S(1)}, bf16[5,8,128]{2,1,0:T(8,128)(2,1)S(1)}, f32[5,16,128]{2,1,0:T(8,128)S(1)}, f32[5,16,128]{2,1,0:T(8,128)S(1)}) custom-call(bf16[4,64,128]{2,1,0:T(8,128)(2,1)S(1)} %copy-done, s32[64,128]{1,0:T(8,128)S(1)} %copy-done.1, bf16[2,5,8,128]{3,2,1,0:T(8,128)(2,1)S(1)} %bitcast.5, ...), custom_call_target="tpu_custom_call" | custom-call | tf_op jit(solution)/shard_map/pack_rows/pallas_call | solution.py:446
  21.3 3.3 %collective-permute-start = (bf16[5,8,128]{2,1,0:T(8,128)(2,1)S(1)}, bf16[5,8,128]{2,1,0:T(8,128)(2,1)S(1)}, u32[]{:S(2)}, u32[]{:S(2)}) collective-permute-start(bf16[5,8,128]{2,1,0:T(8,128)(2,1)S(1)} %get-tuple-element.28), channel_id=1, source_target_pairs={{0,1},{2,3},{4,5},{6,7},{8,9},{10,11},{12,13},{14,15},{16,17},{18,... | collective-permute-start | bytes 30728 | tf_op jit(solution)/shard_map/ppermute | solution.py:569
  24.5 7.1 %all-gather.2 = bf16[10,8,128]{2,1,0:T(8,128)(2,1)S(1)} all-gather(bf16[5,8,128]{2,1,0:T(8,128)(2,1)S(1)} %get-tuple-element.29), channel_id=4, replica_groups={{1,2},{3,4},{5,6},{9,10},{11,12},{13,14},{17,18},{19,20},{21,22},{25,26..., dimensions={0}, use_global_device_ids=true | all-gather | bytes 30720 | tf_op jit(solution)/shard_map/all_gather | solution.py:570
  31.7 0.0 collective-permute-done.lat_in
  31.7 3.1 %edge_lines.1 = f32[2,64,128]{2,1,0:T(8,128)} custom-call(bf16[4,64,128]{2,1,0:T(8,128)(2,1)S(1)} %copy-done, s32[64,128]{1,0:T(8,128)S(1)} %copy-done.1, bf16[2,5,8,128]{3,2,1,0:T(8,128)(2,1)S(1)} %bitcast.6, bf16[2,5,8,128]{3,2,1,0:T(8,128)(2,1)S(1)} %bitcast.8, f32[5,16,128]{2,1,0:T(8,128)S(1)} %get-tuple-element.26.own_low, ...), custom_call_target="tpu_custom_call" | custom-call | tf_op jit(solution)/shard_map/edge_lines/pallas_call | solution.py:526
  (3 shorter events, 0.1 us)
Async XLA Ops:
  0.0 0.8 %copy-start.1 = (s32[64,128]{1,0:T(8,128)S(1)}, s32[64,128]{1,0:T(8,128)}, u32[]{:S(2)}) copy-start(s32[64,128]{1,0:T(8,128)} %mask.9) | copy-start | bytes 98308
  0.7 0.7 %copy-start.6 = (f32[2,128]{1,0:T(2,128)S(1)}, f32[2,128]{1,0:T(2,128)}, u32[]{:S(2)}) copy-start(f32[2,128]{1,0:T(2,128)} %metric.1) | copy-start | bytes 3076
  1.4 2.0 %copy-start = (bf16[4,64,128]{2,1,0:T(8,128)(2,1)S(1)}, bf16[4,64,128]{2,1,0:T(8,128)(2,1)}, u32[]{:S(2)}) copy-start(bf16[4,64,128]{2,1,0:T(8,128)(2,1)} %fields.7) | copy-start | bytes 196612
  1.4 2.0 %copy-start.2 = (bf16[3,5,48,48]{3,2,1,0:T(8,128)(2,1)S(1)}, bf16[3,5,48,48]{3,2,1,0:T(8,128)(2,1)}, u32[]{:S(2)}) copy-start(bf16[3,5,48,48]{3,2,1,0:T(8,128)(2,1)} %w_mid.3) | copy-start | bytes 207364
  1.4 2.0 %copy-start.5 = (f32[4,48]{1,0:T(4,128)S(1)}, f32[4,48]{1,0:T(4,128)}, u32[]{:S(2)}) copy-start(f32[4,48]{1,0:T(4,128)} %biases.3) | copy-start | bytes 2308
  1.4 2.0 %copy-start.4 = (bf16[5,3,48]{2,1,0:T(4,128)(2,1)S(1)}, bf16[5,3,48]{2,1,0:T(4,128)(2,1)}, u32[]{:S(2)}) copy-start(bf16[5,3,48]{2,1,0:T(4,128)(2,1)} %w_last.3) | copy-start | bytes 4324
  3.4 0.7 %copy-start.3 = (bf16[5,48,4]{1,2,0:T(4,128)(2,1)S(1)}, bf16[5,48,4]{1,2,0:T(4,128)(2,1)}, u32[]{:S(2)}) copy-start(bf16[5,48,4]{1,2,0:T(4,128)(2,1)} %param.10) | copy-start | bytes 5764
  21.3 10.4 %collective-permute-start = (bf16[5,8,128]{2,1,0:T(8,128)(2,1)S(1)}, bf16[5,8,128]{2,1,0:T(8,128)(2,1)S(1)}, u32[]{:S(2)}, u32[]{:S(2)}) collective-permute-start(bf16[5,8,128]{2,1,0:T(8,128)(2,1)S(1)} %get-tuple-element.28), channel_id=1, source_target_pairs={{0,1},{2,3},{4,5},{6,7},{8,9},{10,11},{12,13},{14,15},{16,17},{18,... | collective-permute-start | bytes 30728 | tf_op jit(solution)/shard_map/ppermute | solution.py:569
